TPU v7x, 512 devices: a whole 4x4x16 slice. The times are simulated.
512 devices in a mesh: lat: 32 (over z_lo, y), lon: 16 (over z_hi, x, core).
Axes of the slice: x: 4, y: 4, z: 16 (z_hi: 2, z_lo: 8; z = z_hi * 8 + z_lo), core: 2. Of those that a mesh axis runs over, the one named last changes fastest.
Arguments:
- field: float32 [64, 1024, 2048], P(None, 'lat', 'lon'), may hold values from -6 to 6
- cotangent: float32 [64, 1024, 2048], P(None, 'lat', 'lon'), may hold values from -6 to 6
- w_approx: float32 [64, 64, 64, 128], P(None, None, 'lat', 'lon'), may hold values from -0.75 to 0.75
- w_detail: float32 [3, 64, 64, 64, 128], P(None, None, None, 'lat', 'lon'), may hold values from -0.75 to 0.75
- w_point: float32 [64, 64], replicated, may hold values from -0.75 to 0.75
- bias: float32 [64], replicated, may hold values from -4 to 4
Outputs:
- grad_field: float32 [64, 1024, 2048], P(None, 'lat', 'lon')
- grad_approx: float32 [64, 64, 64, 128], P(None, None, 'lat', 'lon')
- grad_detail: float32 [3, 64, 64, 64, 128], P(None, None, None, 'lat', 'lon')
- grad_point: float32 [64, 64], replicated
- grad_bias: float32 [64], replicated
All inputs are finite; a program needn't handle non-finite values.
Results may differ from a plain program's by a relative error of at most 0.00016.
Values sent between devices are 32-bit elements; how exact they have to be, the bound alone decides.
A program may use at most 128 MiB of HBM per device.

v0:
```python
import math

import jax
import jax.numpy as jnp
from jax import lax
from jax.sharding import PartitionSpec as P

low_taps = [
    0.23037781330885523,
    0.7148465705525415,
    0.6308807679295904,
    -0.02798376941698385,
    -0.18703481171888114,
    0.030841381835986965,
    0.032883011666982945,
    -0.010597401784997278,
]
high_taps = [low_taps[7 - j] if j % 2 == 0 else -low_taps[7 - j] for j in range(8)]


def extended_2(block, sides, width):
    for axis, dim in sides:
        count = lax.axis_size(axis)
        forward = [(i, i + 1) for i in range(count - 1)]
        forward.append((count - 1, 0))
        backward = [(target, source) for source, target in forward]
        low = lax.ppermute(
            lax.slice_in_dim(block, block.shape[dim] - width, None, axis=dim), axis, forward
        )
        high = lax.ppermute(lax.slice_in_dim(block, 0, width, axis=dim), axis, backward)
        block = jnp.concatenate([low, block, high], axis=dim)
    return block


def split_axis(extended, axis, count):
    span = 2 * count + 6
    evens = lax.slice_in_dim(extended, 0, span, 2, axis)
    odds = lax.slice_in_dim(extended, 1, span, 2, axis)
    lowpart = None
    highpart = None
    for shift in range(4):
        even_part = lax.slice_in_dim(evens, shift, shift + count, 1, axis)
        odd_part = lax.slice_in_dim(odds, shift, shift + count, 1, axis)
        low_term = low_taps[2 * shift] * even_part + low_taps[2 * shift + 1] * odd_part
        high_term = high_taps[2 * shift] * even_part + high_taps[2 * shift + 1] * odd_part
        lowpart = low_term if lowpart is None else lowpart + low_term
        highpart = high_term if highpart is None else highpart + high_term
    return (lowpart, highpart)


def join_axis(low_ext, high_ext, axis, count):
    evens = None
    odds = None
    for shift in range(4):
        low_part = lax.slice_in_dim(low_ext, 3 - shift, 3 - shift + count, 1, axis)
        high_part = lax.slice_in_dim(high_ext, 3 - shift, 3 - shift + count, 1, axis)
        even_term = low_taps[2 * shift] * low_part + high_taps[2 * shift] * high_part
        odd_term = low_taps[2 * shift + 1] * low_part + high_taps[2 * shift + 1] * high_part
        evens = even_term if evens is None else evens + even_term
        odds = odd_term if odds is None else odds + odd_term
    joined = jnp.stack([evens, odds], axis + 1)
    shape = list(evens.shape)
    shape[axis] = 2 * count
    return joined.reshape(shape)


def split_both(lat_ext, rows, width):
    lowpart, highpart = split_axis(lat_ext, 1, rows)
    bands = []
    for part in (lowpart, highpart):
        lon_ext = lax.slice_in_dim(part, 6, width + 12, 1, 2)
        bands.extend(split_axis(lon_ext, 2, width // 2))
    return bands


def join_both(extended, rows, cols):
    lowpart = join_axis(extended[0], extended[1], 2, cols)
    highpart = join_axis(extended[2], extended[3], 2, cols)
    return join_axis(lowpart, highpart, 1, rows)


def fine_rim(stacked, width):
    return extended_2(stacked, (("lat", 2), ("lon", 3)), width)


def coarse_rim(stacked, width):
    return extended_2(stacked, (("lon", 3),), width)


def fine_split(block):
    height, width = (block.shape[1], block.shape[2])
    extended = fine_rim(block[None], 6)[0]
    lat_ext = lax.slice_in_dim(extended, 6, height + 12, 1, 1)
    return split_both(lat_ext, height // 2, width)


def coarse_split(block):
    height, width = (block.shape[1], block.shape[2])
    extended = coarse_rim(block[None], 6)[0]
    lat_ext = jnp.concatenate([extended, extended[:, :6]], 1)
    return split_both(lat_ext, height // 2, width)


def fine_join(stacked):
    extended = fine_rim(stacked, 3)
    return join_both(extended, stacked.shape[2], stacked.shape[3])


def coarse_join(stacked):
    extended = coarse_rim(stacked, 3)
    extended = jnp.concatenate([extended[:, :, -3:], extended], 2)
    return join_both(extended, stacked.shape[2], stacked.shape[3])


def descend(block, fine_levels):
    details = []
    approx = block
    for level in range(fine_levels):
        bands = fine_split(approx)
        details.append(jnp.stack(bands[1:]))
        approx = bands[0]
    approx = lax.all_to_all(approx, "lat", split_axis=0, concat_axis=1, tiled=True)
    for level in range(4 - fine_levels):
        bands = coarse_split(approx)
        details.append(jnp.stack(bands[1:]))
        approx = bands[0]
    coarse = jnp.concatenate([approx[None], details[3]], 0)
    coarse = lax.all_to_all(coarse, "lat", split_axis=2, concat_axis=1, tiled=True)
    return (coarse, details)


def ascend(mixed_own, details, fine_levels):
    mixed = lax.all_to_all(mixed_own, "lat", split_axis=1, concat_axis=2, tiled=True)
    approx = coarse_join(mixed)
    level = 2
    approx = coarse_join(jnp.concatenate([approx[None], details[level]], 0))
    approx = lax.all_to_all(approx, "lat", split_axis=1, concat_axis=0, tiled=True)
    for level in range(fine_levels - 1, -1, -1):
        approx = fine_join(jnp.concatenate([approx[None], details[level]], 0))
    return approx


def body(field, cotangent, w_approx, w_detail, w_point, bias):
    fine_levels = 2
    highest = lax.Precision.HIGHEST
    weights = jnp.concatenate([w_approx[None], w_detail], 0)
    coarse, details = descend(field, fine_levels)
    mixed_own = jnp.einsum("bcij,bcoij->boij", coarse, weights, precision=highest)
    branch = ascend(mixed_own, details, fine_levels)
    pointwise = jnp.einsum("oc,chw->ohw", w_point, field, precision=highest)
    pre = branch + pointwise + bias[:, None, None]
    normal_cdf = 0.5 * (1.0 + lax.erf(pre / math.sqrt(2.0)))
    normal_pdf = jnp.exp(-0.5 * pre * pre) / math.sqrt(2.0 * math.pi)
    hgrad = cotangent * (normal_cdf + pre * normal_pdf)
    point_term = jnp.einsum("ohw,chw->oc", hgrad, field, precision=highest)
    bias_term = jnp.sum(hgrad, axis=(1, 2))
    grad_point, grad_bias = lax.psum((point_term, bias_term), ("lat", "lon"))
    gcoarse, gdetails = descend(hgrad, fine_levels)
    gweights = jnp.einsum("bcij,boij->bcoij", coarse, gcoarse)
    back_own = jnp.einsum("bcoij,boij->bcij", weights, gcoarse, precision=highest)
    grad_branch = ascend(back_own, gdetails, fine_levels)
    grad_field = grad_branch + jnp.einsum("oc,ohw->chw", w_point, hgrad, precision=highest)
    return (grad_field, gweights[0], gweights[1:], grad_point, grad_bias)


def solution(mesh):
    placed = (
        P(None, "lat", "lon"),
        P(None, "lat", "lon"),
        P(None, None, "lat", "lon"),
        P(None, None, None, "lat", "lon"),
        P(),
        P(),
    )
    return jax.shard_map(
        body,
        mesh=mesh,
        in_specs=placed,
        out_specs=(
            P(None, "lat", "lon"),
            P(None, None, "lat", "lon"),
            P(None, None, None, "lat", "lon"),
            P(),
            P(),
        ),
        check_vma=False,
    )
```

profile of v0, /device:TPU:7, one launch (start us, length us, event | category | flops | bytes accessed | tf_op | source)
XLA Modules:
  0.0 1034.4 jit_solution(8441810868094454342)
XLA Ops:
  5.7 14.0 %collective-permute-start.1 = (f32[1,64,6,128]{3,1,2,0:T(8,128)S(1)}, f32[1,64,6,128]{3,1,2,0:T(8,128)S(1)}, u32[]{:S(2)}, u32[]{:S(2)}) collective-permute-start(f32[1,64,6,128]{3,1,2,0:T(8,128)S(1)} %get-tuple-element.134), channel_id=1, source_target_pairs={{16,0},{32,16},{48,32},{64,48},{80,64},{96,80},{112,96},{128,112},... | collective-permute-start | bytes 589832 | tf_op jit(solution)/shard_map/ppermute | solution.py:30
  26.9 13.5 %collective-permute-start.2 = (f32[1,64,44,6]{1,0,3,2:T(1,128)S(1)}, f32[1,64,44,6]{1,0,3,2:T(1,128)S(1)}, u32[]{:S(2)}, u32[]{:S(2)}) collective-permute-start(f32[1,64,44,6]{1,0,3,2:T(1,128)S(1)} %copy.655), channel_id=1, source_target_pairs={{0,1},{1,2},{2,3},{3,4},{4,5},{5,6},{6,7},{7,8},{8,9},{9,10},{10,1... | collective-permute-start | bytes 202760 | tf_op jit(solution)/shard_map/ppermute | solution.py:27
  43.4 14.7 %collective-permute-done.3 = f32[1,64,44,6]{1,0,3,2:T(1,128)S(1)} collective-permute-done((f32[1,64,44,6]{1,0,3,2:T(1,128)S(1)}, f32[1,64,44,6]{1,0,3,2:T(1,128)S(1)}, u32[]{:S(2)}, u32[]{:S(2)}) %collective-permute-start.3) | collective-permute-done | bytes 67616 | tf_op jit(solution)/shard_map/ppermute | solution.py:30
  67.0 9.3 slice.1642
  76.3 9.5 slice.1644
  88.7 13.0 %collective-permute-start.5 = (f32[1,64,6,64]{3,1,2,0:T(8,128)S(1)}, f32[1,64,6,64]{3,1,2,0:T(8,128)S(1)}, u32[]{:S(2)}, u32[]{:S(2)}) collective-permute-start(f32[1,64,6,64]{3,1,2,0:T(8,128)S(1)} %get-tuple-element.166), channel_id=1, source_target_pairs={{16,0},{32,16},{48,32},{64,48},{80,64},{96,80},{112,96},{128,112},... | collective-permute-start | bytes 294920 | tf_op jit(solution)/shard_map/ppermute | solution.py:30
  112.3 14.4 %collective-permute-done.7 = f32[1,64,28,6]{1,0,3,2:T(1,128)} collective-permute-done((f32[1,64,28,6]{1,0,3,2:T(1,128)S(1)}, f32[1,64,28,6]{1,0,3,2:T(1,128)}, u32[]{:S(2)}, u32[]{:S(2)}) %collective-permute-start.7) | collective-permute-done | bytes 43040 | tf_op jit(solution)/shard_map/ppermute | solution.py:30
  135.5 24.1 %all_to_all.138 = f32[32,1,512]{2,1,0:T(1,128)S(1)} all-to-all(f32[32,1,512]{2,1,0:T(1,128)S(1)} %reshape.102), channel_id=1, replica_groups=mesh['lat'=32,'lon'=16] {'lat'}, dimensions={0} | all-to-all | bytes 131072 | tf_op jit(solution)/shard_map/all_to_all | solution.py:122
  166.3 13.9 %collective-permute-done.9 = f32[1,2,256,6]{2,3,1,0:T(8,128)S(1)} collective-permute-done((f32[1,2,256,6]{2,3,1,0:T(8,128)S(1)}, f32[1,2,256,6]{2,3,1,0:T(8,128)S(1)}, u32[]{:S(2)}, u32[]{:S(2)}) %collective-permute-start.9) | collective-permute-done | bytes 12320 | tf_op jit(solution)/shard_map/ppermute | solution.py:30
  188.2 13.4 %collective-permute-done.11 = f32[1,2,128,6]{2,3,1,0:T(8,128)S(1)} collective-permute-done((f32[1,2,128,6]{2,3,1,0:T(8,128)S(1)}, f32[1,2,128,6]{2,3,1,0:T(8,128)S(1)}, u32[]{:S(2)}, u32[]{:S(2)}) %collective-permute-start.11) | collective-permute-done | bytes 6176 | tf_op jit(solution)/shard_map/ppermute | solution.py:30
  203.9 14.9 %all_to_all.139 = f32[32,1,128]{2,1,0:T(1,128)S(1)} all-to-all(f32[32,1,128]{2,1,0:T(1,128)S(1)} %reshape.104), channel_id=1, replica_groups=mesh['lat'=32,'lon'=16] {'lat'}, dimensions={0} | all-to-all | bytes 32768 | tf_op jit(solution)/shard_map/all_to_all | solution.py:128
  226.2 11.3 %all-to-all-done.2 = f32[32,1,128]{2,1,0:T(1,128)S(1)} async-done(((f32[32,1,128]{2,1,0:T(1,128)}), f32[32,1,128]{2,1,0:T(1,128)S(1)}, u32[]{:S(2)}, u32[]{:S(2)}) %all-to-all-start.2) | async-done | bytes 16416 | tf_op jit(solution)/shard_map/all_to_all | solution.py:133
  239.1 4.5 collective-permute-start.12
  250.1 15.2 %collective-permute-done.13 = f32[4,2,64,3]{3,2,1,0:T(8,128)S(1)} collective-permute-done((f32[4,2,64,3]{3,2,1,0:T(8,128)S(1)}, f32[4,2,64,3]{3,2,1,0:T(8,128)S(1)}, u32[]{:S(2)}, u32[]{:S(2)}) %collective-permute-start.13) | collective-permute-done | bytes 6176 | tf_op jit(solution)/shard_map/ppermute | solution.py:30
  270.5 13.4 %collective-permute-done.15 = f32[4,2,128,3]{2,3,1,0:T(4,128)S(1)} collective-permute-done((f32[4,2,128,3]{2,3,1,0:T(4,128)S(1)}, f32[4,2,128,3]{2,3,1,0:T(4,128)S(1)}, u32[]{:S(2)}, u32[]{:S(2)}) %collective-permute-start.15) | collective-permute-done | bytes 12320 | tf_op jit(solution)/shard_map/ppermute | solution.py:30
  286.6 7.9 all-to-all-start.3
  300.1 6.2 all-to-all-done.3
  310.8 12.2 %collective-permute-start.17 = (f32[4,64,3,32]{3,1,2,0:T(8,128)}, f32[4,64,3,32]{3,1,2,0:T(8,128)S(1)}, u32[]{:S(2)}, u32[]{:S(2)}) collective-permute-start(f32[4,64,3,32]{3,1,2,0:T(8,128)} %get-tuple-element.128), channel_id=1, source_target_pairs={{16,0},{32,16},{48,32},{64,48},{80,64},{96,80},{112,96},{128,112},... | collective-permute-start | bytes 294920 | tf_op jit(solution)/shard_map/ppermute | solution.py:30
  323.0 10.2 slice.1854
  333.2 10.3 %slice.1856 = f32[64,16,67]{2,0,1:T(8,128)S(1)} slice(f32[64,16,134]{2,0,1:T(8,128)} %get-tuple-element.50), slice={[0:64:1], [0:16:1], [1:134:2]} | slice | bytes 548864 | tf_op jit(solution)/shard_map/slice | solution.py:38
  360.3 10.9 %collective-permute-done.19 = f32[4,64,14,3]{1,0,3,2:T(4,128)} collective-permute-done((f32[4,64,14,3]{1,0,3,2:T(4,128)}, f32[4,64,14,3]{1,0,3,2:T(4,128)}, u32[]{:S(2)}, u32[]{:S(2)}) %collective-permute-start.19) | collective-permute-done | bytes 43040 | tf_op jit(solution)/shard_map/ppermute | solution.py:30
  386.3 12.2 %collective-permute-start.21 = (f32[4,64,3,64]{3,1,2,0:T(8,128)S(1)}, f32[4,64,3,64]{3,1,2,0:T(8,128)S(1)}, u32[]{:S(2)}, u32[]{:S(2)}) collective-permute-start(f32[4,64,3,64]{3,1,2,0:T(8,128)S(1)} %get-tuple-element.76), channel_id=1, source_target_pairs={{16,0},{32,16},{48,32},{64,48},{80,64},{96,80},{112,96},{128,112},... | collective-permute-start | bytes 589832 | tf_op jit(solution)/shard_map/ppermute | solution.py:30
  420.1 13.6 %collective-permute-done.23 = f32[4,64,22,3]{1,0,3,2:T(4,128)} collective-permute-done((f32[4,64,22,3]{1,0,3,2:T(4,128)}, f32[4,64,22,3]{1,0,3,2:T(4,128)}, u32[]{:S(2)}, u32[]{:S(2)}) %collective-permute-start.23) | collective-permute-done | bytes 67616 | tf_op jit(solution)/shard_map/ppermute | solution.py:30
  460.8 13.0 %collective-permute-start.25 = (f32[1,64,6,128]{3,1,2,0:T(8,128)S(1)}, f32[1,64,6,128]{3,1,2,0:T(8,128)S(1)}, u32[]{:S(2)}, u32[]{:S(2)}) collective-permute-start(f32[1,64,6,128]{3,1,2,0:T(8,128)S(1)} %get-tuple-element.126), channel_id=1, source_target_pairs={{16,0},{32,16},{48,32},{64,48},{80,64},{96,80},{112,96},{128,112},... | collective-permute-start | bytes 589832 | tf_op jit(solution)/shard_map/ppermute | solution.py:30
  489.2 13.6 %collective-permute-done.27 = f32[1,64,44,6]{1,0,3,2:T(1,128)S(1)} collective-permute-done((f32[1,64,44,6]{1,0,3,2:T(1,128)S(1)}, f32[1,64,44,6]{1,0,3,2:T(1,128)S(1)}, u32[]{:S(2)}, u32[]{:S(2)}) %collective-permute-start.27) | collective-permute-done | bytes 67616 | tf_op jit(solution)/shard_map/ppermute | solution.py:30
  512.4 10.2 slice.1912
  522.7 10.3 %slice.1914 = f32[64,16,67]{2,0,1:T(8,128)S(1)} slice(f32[64,16,134]{2,0,1:T(8,128)} %get-tuple-element.47), slice={[0:64:1], [0:16:1], [1:134:2]} | slice | bytes 548864 | tf_op jit(solution)/shard_map/slice | solution.py:38
  536.7 12.8 %collective-permute-start.29 = (f32[1,64,6,64]{3,1,2,0:T(8,128)S(1)}, f32[1,64,6,64]{3,1,2,0:T(8,128)S(1)}, u32[]{:S(2)}, u32[]{:S(2)}) collective-permute-start(f32[1,64,6,64]{3,1,2,0:T(8,128)S(1)} %get-tuple-element.160), channel_id=1, source_target_pairs={{16,0},{32,16},{48,32},{64,48},{80,64},{96,80},{112,96},{128,112},... | collective-permute-start | bytes 294920 | tf_op jit(solution)/shard_map/ppermute | solution.py:30
  564.2 13.0 %collective-permute-done.31 = f32[1,64,28,6]{1,0,3,2:T(1,128)S(1)} collective-permute-done((f32[1,64,28,6]{1,0,3,2:T(1,128)S(1)}, f32[1,64,28,6]{1,0,3,2:T(1,128)S(1)}, u32[]{:S(2)}, u32[]{:S(2)}) %collective-permute-start.31) | collective-permute-done | bytes 43040 | tf_op jit(solution)/shard_map/ppermute | solution.py:30
  587.4 24.1 %all_to_all.140 = f32[32,1,512]{2,1,0:T(1,128)S(1)} all-to-all(f32[32,1,512]{2,1,0:T(1,128)S(1)} %reshape.110), channel_id=1, replica_groups=mesh['lat'=32,'lon'=16] {'lat'}, dimensions={0} | all-to-all | bytes 131072 | tf_op jit(solution)/shard_map/all_to_all | solution.py:122
  617.8 13.9 %collective-permute-done.33 = f32[1,2,256,6]{2,3,1,0:T(8,128)S(1)} collective-permute-done((f32[1,2,256,6]{2,3,1,0:T(8,128)S(1)}, f32[1,2,256,6]{2,3,1,0:T(8,128)S(1)}, u32[]{:S(2)}, u32[]{:S(2)}) %collective-permute-start.33) | collective-permute-done | bytes 12320 | tf_op jit(solution)/shard_map/ppermute | solution.py:30
  639.9 13.4 %collective-permute-done.35 = f32[1,2,128,6]{2,3,1,0:T(8,128)S(1)} collective-permute-done((f32[1,2,128,6]{2,3,1,0:T(8,128)S(1)}, f32[1,2,128,6]{2,3,1,0:T(8,128)S(1)}, u32[]{:S(2)}, u32[]{:S(2)}) %collective-permute-start.35) | collective-permute-done | bytes 6176 | tf_op jit(solution)/shard_map/ppermute | solution.py:30
  655.6 14.8 %all_to_all.141 = f32[32,1,128]{2,1,0:T(1,128)S(1)} all-to-all(f32[32,1,128]{2,1,0:T(1,128)S(1)} %reshape.112), channel_id=1, replica_groups=mesh['lat'=32,'lon'=16] {'lat'}, dimensions={0} | all-to-all | bytes 32768 | tf_op jit(solution)/shard_map/all_to_all | solution.py:128
  680.5 11.3 %all-to-all-done.6 = f32[32,1,128]{2,1,0:T(1,128)S(1)} async-done(((f32[32,1,128]{2,1,0:T(1,128)}), f32[32,1,128]{2,1,0:T(1,128)S(1)}, u32[]{:S(2)}, u32[]{:S(2)}) %all-to-all-start.6) | async-done | bytes 16416 | tf_op jit(solution)/shard_map/all_to_all | solution.py:133
  700.6 4.7 collective-permute-done.36
  705.4 15.1 %collective-permute-done.37 = f32[4,2,64,3]{3,2,1,0:T(8,128)S(1)} collective-permute-done((f32[4,2,64,3]{3,2,1,0:T(8,128)}, f32[4,2,64,3]{3,2,1,0:T(8,128)S(1)}, u32[]{:S(2)}, u32[]{:S(2)}) %collective-permute-start.37) | collective-permute-done | bytes 6176 | tf_op jit(solution)/shard_map/ppermute | solution.py:30
  725.8 13.4 %collective-permute-done.39 = f32[4,2,128,3]{2,3,1,0:T(4,128)S(1)} collective-permute-done((f32[4,2,128,3]{2,3,1,0:T(4,128)S(1)}, f32[4,2,128,3]{2,3,1,0:T(4,128)S(1)}, u32[]{:S(2)}, u32[]{:S(2)}) %collective-permute-start.39) | collective-permute-done | bytes 12320 | tf_op jit(solution)/shard_map/ppermute | solution.py:30
  741.9 7.8 all-to-all-start.7
  755.3 6.2 all-to-all-done.7
  766.0 12.0 %collective-permute-start.41 = (f32[4,64,3,32]{3,1,2,0:T(8,128)}, f32[4,64,3,32]{3,1,2,0:T(8,128)}, u32[]{:S(2)}, u32[]{:S(2)}) collective-permute-start(f32[4,64,3,32]{3,1,2,0:T(8,128)} %get-tuple-element.120), channel_id=1, source_target_pairs={{16,0},{32,16},{48,32},{64,48},{80,64},{96,80},{112,96},{128,112},... | collective-permute-start | bytes 294920 | tf_op jit(solution)/shard_map/ppermute | solution.py:30
  778.0 10.2 slice.2124
  788.2 10.3 %slice.2126 = f32[64,16,67]{2,0,1:T(8,128)S(1)} slice(f32[64,16,134]{2,0,1:T(8,128)} %get-tuple-element.48), slice={[0:64:1], [0:16:1], [1:134:2]} | slice | bytes 548864 | tf_op jit(solution)/shard_map/slice | solution.py:38
  817.9 10.3 collective-permute-done.43
  849.1 12.3 %collective-permute-start.45 = (f32[4,64,3,64]{3,1,2,0:T(8,128)}, f32[4,64,3,64]{3,1,2,0:T(8,128)}, u32[]{:S(2)}, u32[]{:S(2)}) collective-permute-start(f32[4,64,3,64]{3,1,2,0:T(8,128)} %get-tuple-element.72), channel_id=1, source_target_pairs={{16,0},{32,16},{48,32},{64,48},{80,64},{96,80},{112,96},{128,112},... | collective-permute-start | bytes 589832 | tf_op jit(solution)/shard_map/ppermute | solution.py:30
  863.0 99.6 %all-reduce = (f32[64,64]{1,0:T(8,128)}, f32[64]{0:T(128)}) all-reduce(f32[64,64]{1,0:T(8,128)S(1)} %convolution_bitcast_fusion.1, f32[64]{0:T(128)S(1)} %get-tuple-element.297), channel_id=1, replica_groups=mesh['lat'=32,'lon'=16] {'lat','lon'}, use_global_device_ids=true, to_apply=%region_0.0 | all-reduce | flops 4160 | bytes 33280 | tf_op jit(solution)/shard_map/psum | solution.py:157
  970.2 7.6 collective-permute-start.46
  987.0 15.5 %collective-permute-done.47 = f32[4,64,22,3]{1,0,3,2:T(4,128)} collective-permute-done((f32[4,64,22,3]{1,0,3,2:T(4,128)}, f32[4,64,22,3]{1,0,3,2:T(4,128)}, u32[]{:S(2)}, u32[]{:S(2)}) %collective-permute-start.47) | collective-permute-done | bytes 67616 | tf_op jit(solution)/shard_map/ppermute | solution.py:30
  1005.6 4.7 pad_maximum_fusion.3
  (497 shorter events, 367.3 us)
Async XLA Ops:
  2.5 19.9 %collective-permute-start = (f32[1,64,6,128]{3,1,2,0:T(8,128)S(1)}, f32[1,64,6,128]{3,1,2,0:T(8,128)S(1)}, u32[]{:S(2)}, u32[]{:S(2)}) collective-permute-start(f32[1,64,6,128]{3,1,2,0:T(8,128)S(1)} %get-tuple-element.133), channel_id=1, source_target_pairs={{0,16},{16,32},{32,48},{48,64},{64,80},{80,96},{96,112},{112,128},... | collective-permute-start | bytes 589832 | tf_op jit(solution)/shard_map/ppermute | solution.py:27
  5.7 17.6 %collective-permute-start.1 = (f32[1,64,6,128]{3,1,2,0:T(8,128)S(1)}, f32[1,64,6,128]{3,1,2,0:T(8,128)S(1)}, u32[]{:S(2)}, u32[]{:S(2)}) collective-permute-start(f32[1,64,6,128]{3,1,2,0:T(8,128)S(1)} %get-tuple-element.134), channel_id=1, source_target_pairs={{16,0},{32,16},{48,32},{64,48},{80,64},{96,80},{112,96},{128,112},... | collective-permute-start | bytes 589832 | tf_op jit(solution)/shard_map/ppermute | solution.py:30
  26.9 16.0 %collective-permute-start.2 = (f32[1,64,44,6]{1,0,3,2:T(1,128)S(1)}, f32[1,64,44,6]{1,0,3,2:T(1,128)S(1)}, u32[]{:S(2)}, u32[]{:S(2)}) collective-permute-start(f32[1,64,44,6]{1,0,3,2:T(1,128)S(1)} %copy.655), channel_id=1, source_target_pairs={{0,1},{1,2},{2,3},{3,4},{4,5},{5,6},{6,7},{7,8},{8,9},{9,10},{10,1... | collective-permute-start | bytes 202760 | tf_op jit(solution)/shard_map/ppermute | solution.py:27
  41.0 17.2 %collective-permute-start.3 = (f32[1,64,44,6]{1,0,3,2:T(1,128)S(1)}, f32[1,64,44,6]{1,0,3,2:T(1,128)S(1)}, u32[]{:S(2)}, u32[]{:S(2)}) collective-permute-start(f32[1,64,44,6]{1,0,3,2:T(1,128)S(1)} %copy.656), channel_id=1, source_target_pairs={{1,0},{2,1},{3,2},{4,3},{5,4},{6,5},{7,6},{8,7},{9,8},{10,9},{11,1... | collective-permute-start | bytes 202760 | tf_op jit(solution)/shard_map/ppermute | solution.py:30
  86.8 16.8 %collective-permute-start.4 = (f32[1,64,6,64]{3,1,2,0:T(8,128)S(1)}, f32[1,64,6,64]{3,1,2,0:T(8,128)S(1)}, u32[]{:S(2)}, u32[]{:S(2)}) collective-permute-start(f32[1,64,6,64]{3,1,2,0:T(8,128)S(1)} %get-tuple-element.165), channel_id=1, source_target_pairs={{0,16},{16,32},{32,48},{48,64},{64,80},{80,96},{96,112},{112,128},... | collective-permute-start | bytes 294920 | tf_op jit(solution)/shard_map/ppermute | solution.py:27
  88.7 15.4 %collective-permute-start.5 = (f32[1,64,6,64]{3,1,2,0:T(8,128)S(1)}, f32[1,64,6,64]{3,1,2,0:T(8,128)S(1)}, u32[]{:S(2)}, u32[]{:S(2)}) collective-permute-start(f32[1,64,6,64]{3,1,2,0:T(8,128)S(1)} %get-tuple-element.166), channel_id=1, source_target_pairs={{16,0},{32,16},{48,32},{64,48},{80,64},{96,80},{112,96},{128,112},... | collective-permute-start | bytes 294920 | tf_op jit(solution)/shard_map/ppermute | solution.py:30
  107.0 4.9 collective-permute-start.6
  110.0 16.7 %collective-permute-start.7 = (f32[1,64,28,6]{1,0,3,2:T(1,128)S(1)}, f32[1,64,28,6]{1,0,3,2:T(1,128)}, u32[]{:S(2)}, u32[]{:S(2)}) collective-permute-start(f32[1,64,28,6]{1,0,3,2:T(1,128)S(1)} %copy.660), channel_id=1, source_target_pairs={{1,0},{2,1},{3,2},{4,3},{5,4},{6,5},{7,6},{8,7},{9,8},{10,9},{11,1... | collective-permute-start | bytes 129032 | tf_op jit(solution)/shard_map/ppermute | solution.py:30
  161.2 5.1 collective-permute-start.8
  164.3 15.9 %collective-permute-start.9 = (f32[1,2,256,6]{2,3,1,0:T(8,128)S(1)}, f32[1,2,256,6]{2,3,1,0:T(8,128)S(1)}, u32[]{:S(2)}, u32[]{:S(2)}) collective-permute-start(f32[1,2,256,6]{2,3,1,0:T(8,128)S(1)} %get-tuple-element.238), channel_id=1, source_target_pairs={{1,0},{2,1},{3,2},{4,3},{5,4},{6,5},{7,6},{8,7},{9,8},{10,9},{11,1... | collective-permute-start | bytes 36872 | tf_op jit(solution)/shard_map/ppermute | solution.py:30
  185.8 15.8 %collective-permute-start.11 = (f32[1,2,128,6]{2,3,1,0:T(8,128)S(1)}, f32[1,2,128,6]{2,3,1,0:T(8,128)S(1)}, u32[]{:S(2)}, u32[]{:S(2)}) collective-permute-start(f32[1,2,128,6]{2,3,1,0:T(8,128)S(1)} %get-tuple-element.296), channel_id=1, source_target_pairs={{1,0},{2,1},{3,2},{4,3},{5,4},{6,5},{7,6},{8,7},{9,8},{10,9},{11,1... | collective-permute-start | bytes 18440 | tf_op jit(solution)/shard_map/ppermute | solution.py:30
  222.4 15.2 %all-to-all-start.2 = ((f32[32,1,128]{2,1,0:T(1,128)}), f32[32,1,128]{2,1,0:T(1,128)S(1)}, u32[]{:S(2)}, u32[]{:S(2)}) async-start(f32[32,1,128]{2,1,0:T(1,128)} %reshape.106), calls=%async_computation.2 | async-start | bytes 32768 | tf_op jit(solution)/shard_map/all_to_all | solution.py:133
  239.1 10.9 %collective-permute-start.12 = (f32[4,2,64,3]{3,2,1,0:T(8,128)S(1)}, f32[4,2,64,3]{3,2,1,0:T(8,128)S(1)}, u32[]{:S(2)}, u32[]{:S(2)}) collective-permute-start(f32[4,2,64,3]{3,2,1,0:T(8,128)S(1)} %get-tuple-element.189), channel_id=1, source_target_pairs={{0,1},{1,2},{2,3},{3,4},{4,5},{5,6},{6,7},{7,8},{8,9},{9,10},{10,1... | collective-permute-start | bytes 18440 | tf_op jit(solution)/shard_map/ppermute | solution.py:27
  243.6 21.7 %collective-permute-start.13 = (f32[4,2,64,3]{3,2,1,0:T(8,128)S(1)}, f32[4,2,64,3]{3,2,1,0:T(8,128)S(1)}, u32[]{:S(2)}, u32[]{:S(2)}) collective-permute-start(f32[4,2,64,3]{3,2,1,0:T(8,128)S(1)} %get-tuple-element.190), channel_id=1, source_target_pairs={{1,0},{2,1},{3,2},{4,3},{5,4},{6,5},{7,6},{8,7},{9,8},{10,9},{11,1... | collective-permute-start | bytes 18440 | tf_op jit(solution)/shard_map/ppermute | solution.py:30
  268.0 15.9 %collective-permute-start.15 = (f32[4,2,128,3]{2,3,1,0:T(4,128)S(1)}, f32[4,2,128,3]{2,3,1,0:T(4,128)S(1)}, u32[]{:S(2)}, u32[]{:S(2)}) collective-permute-start(f32[4,2,128,3]{2,3,1,0:T(4,128)S(1)} %get-tuple-element.235), channel_id=1, source_target_pairs={{1,0},{2,1},{3,2},{4,3},{5,4},{6,5},{7,6},{8,7},{9,8},{10,9},{11,1... | collective-permute-start | bytes 36872 | tf_op jit(solution)/shard_map/ppermute | solution.py:30
  286.6 19.7 %all-to-all-start.3 = ((f32[32,1,512]{2,1,0:T(1,128)}), f32[32,1,512]{2,1,0:T(1,128)S(1)}, u32[]{:S(2)}, u32[]{:S(2)}) async-start(f32[32,1,512]{2,1,0:T(1,128)} %reshape.108), calls=%async_computation.3 | async-start | bytes 131072 | tf_op jit(solution)/shard_map/all_to_all | solution.py:137
  308.6 35.0 %collective-permute-start.16 = (f32[4,64,3,32]{3,1,2,0:T(8,128)}, f32[4,64,3,32]{3,1,2,0:T(8,128)S(1)}, u32[]{:S(2)}, u32[]{:S(2)}) collective-permute-start(f32[4,64,3,32]{3,1,2,0:T(8,128)} %get-tuple-element.127), channel_id=1, source_target_pairs={{0,16},{16,32},{32,48},{48,64},{64,80},{80,96},{96,112},{112,128},... | collective-permute-start | bytes 294920 | tf_op jit(solution)/shard_map/ppermute | solution.py:27
  310.8 32.8 %collective-permute-start.17 = (f32[4,64,3,32]{3,1,2,0:T(8,128)}, f32[4,64,3,32]{3,1,2,0:T(8,128)S(1)}, u32[]{:S(2)}, u32[]{:S(2)}) collective-permute-start(f32[4,64,3,32]{3,1,2,0:T(8,128)} %get-tuple-element.128), channel_id=1, source_target_pairs={{16,0},{32,16},{48,32},{64,48},{80,64},{96,80},{112,96},{128,112},... | collective-permute-start | bytes 294920 | tf_op jit(solution)/shard_map/ppermute | solution.py:30
  349.2 7.9 collective-permute-start.18
  354.2 16.9 %collective-permute-start.19 = (f32[4,64,14,3]{1,0,3,2:T(4,128)}, f32[4,64,14,3]{1,0,3,2:T(4,128)}, u32[]{:S(2)}, u32[]{:S(2)}) collective-permute-start(f32[4,64,14,3]{1,0,3,2:T(4,128)} %copy.703), channel_id=1, source_target_pairs={{1,0},{2,1},{3,2},{4,3},{5,4},{6,5},{7,6},{8,7},{9,8},{10,9},{11,1... | collective-permute-start | bytes 129032 | tf_op jit(solution)/shard_map/ppermute | solution.py:30
  384.4 17.2 %collective-permute-start.20 = (f32[4,64,3,64]{3,1,2,0:T(8,128)S(1)}, f32[4,64,3,64]{3,1,2,0:T(8,128)S(1)}, u32[]{:S(2)}, u32[]{:S(2)}) collective-permute-start(f32[4,64,3,64]{3,1,2,0:T(8,128)S(1)} %get-tuple-element.75), channel_id=1, source_target_pairs={{0,16},{16,32},{32,48},{48,64},{64,80},{80,96},{96,112},{112,128},... | collective-permute-start | bytes 589832 | tf_op jit(solution)/shard_map/ppermute | solution.py:27
  386.3 17.4 %collective-permute-start.21 = (f32[4,64,3,64]{3,1,2,0:T(8,128)S(1)}, f32[4,64,3,64]{3,1,2,0:T(8,128)S(1)}, u32[]{:S(2)}, u32[]{:S(2)}) collective-permute-start(f32[4,64,3,64]{3,1,2,0:T(8,128)S(1)} %get-tuple-element.76), channel_id=1, source_target_pairs={{16,0},{32,16},{48,32},{64,48},{80,64},{96,80},{112,96},{128,112},... | collective-permute-start | bytes 589832 | tf_op jit(solution)/shard_map/ppermute | solution.py:30
  410.4 7.8 collective-permute-start.22
  416.3 17.5 %collective-permute-start.23 = (f32[4,64,22,3]{1,0,3,2:T(4,128)}, f32[4,64,22,3]{1,0,3,2:T(4,128)}, u32[]{:S(2)}, u32[]{:S(2)}) collective-permute-start(f32[4,64,22,3]{1,0,3,2:T(4,128)} %copy.710), channel_id=1, source_target_pairs={{1,0},{2,1},{3,2},{4,3},{5,4},{6,5},{7,6},{8,7},{9,8},{10,9},{11,1... | collective-permute-start | bytes 202760 | tf_op jit(solution)/shard_map/ppermute | solution.py:30
  458.9 17.4 %collective-permute-start.24 = (f32[1,64,6,128]{3,1,2,0:T(8,128)S(1)}, f32[1,64,6,128]{3,1,2,0:T(8,128)S(1)}, u32[]{:S(2)}, u32[]{:S(2)}) collective-permute-start(f32[1,64,6,128]{3,1,2,0:T(8,128)S(1)} %get-tuple-element.125), channel_id=1, source_target_pairs={{0,16},{16,32},{32,48},{48,64},{64,80},{80,96},{96,112},{112,128},... | collective-permute-start | bytes 589832 | tf_op jit(solution)/shard_map/ppermute | solution.py:27
  460.8 15.5 %collective-permute-start.25 = (f32[1,64,6,128]{3,1,2,0:T(8,128)S(1)}, f32[1,64,6,128]{3,1,2,0:T(8,128)S(1)}, u32[]{:S(2)}, u32[]{:S(2)}) collective-permute-start(f32[1,64,6,128]{3,1,2,0:T(8,128)S(1)} %get-tuple-element.126), channel_id=1, source_target_pairs={{16,0},{32,16},{48,32},{64,48},{80,64},{96,80},{112,96},{128,112},... | collective-permute-start | bytes 589832 | tf_op jit(solution)/shard_map/ppermute | solution.py:30
  480.3 7.2 collective-permute-start.26
  485.6 17.2 %collective-permute-start.27 = (f32[1,64,44,6]{1,0,3,2:T(1,128)S(1)}, f32[1,64,44,6]{1,0,3,2:T(1,128)S(1)}, u32[]{:S(2)}, u32[]{:S(2)}) collective-permute-start(f32[1,64,44,6]{1,0,3,2:T(1,128)S(1)} %copy.719), channel_id=1, source_target_pairs={{1,0},{2,1},{3,2},{4,3},{5,4},{6,5},{7,6},{8,7},{9,8},{10,9},{11,1... | collective-permute-start | bytes 202760 | tf_op jit(solution)/shard_map/ppermute | solution.py:30
  534.7 15.9 %collective-permute-start.28 = (f32[1,64,6,64]{3,1,2,0:T(8,128)S(1)}, f32[1,64,6,64]{3,1,2,0:T(8,128)S(1)}, u32[]{:S(2)}, u32[]{:S(2)}) collective-permute-start(f32[1,64,6,64]{3,1,2,0:T(8,128)S(1)} %get-tuple-element.159), channel_id=1, source_target_pairs={{0,16},{16,32},{32,48},{48,64},{64,80},{80,96},{96,112},{112,128},... | collective-permute-start | bytes 294920 | tf_op jit(solution)/shard_map/ppermute | solution.py:27
  536.7 15.4 %collective-permute-start.29 = (f32[1,64,6,64]{3,1,2,0:T(8,128)S(1)}, f32[1,64,6,64]{3,1,2,0:T(8,128)S(1)}, u32[]{:S(2)}, u32[]{:S(2)}) collective-permute-start(f32[1,64,6,64]{3,1,2,0:T(8,128)S(1)} %get-tuple-element.160), channel_id=1, source_target_pairs={{16,0},{32,16},{48,32},{64,48},{80,64},{96,80},{112,96},{128,112},... | collective-permute-start | bytes 294920 | tf_op jit(solution)/shard_map/ppermute | solution.py:30
  556.0 6.9 collective-permute-start.30
  560.6 16.6 %collective-permute-start.31 = (f32[1,64,28,6]{1,0,3,2:T(1,128)S(1)}, f32[1,64,28,6]{1,0,3,2:T(1,128)S(1)}, u32[]{:S(2)}, u32[]{:S(2)}) collective-permute-start(f32[1,64,28,6]{1,0,3,2:T(1,128)S(1)} %copy.723), channel_id=1, source_target_pairs={{1,0},{2,1},{3,2},{4,3},{5,4},{6,5},{7,6},{8,7},{9,8},{10,9},{11,1... | collective-permute-start | bytes 129032 | tf_op jit(solution)/shard_map/ppermute | solution.py:30
  612.6 5.2 collective-permute-start.32
  615.9 15.9 %collective-permute-start.33 = (f32[1,2,256,6]{2,3,1,0:T(8,128)S(1)}, f32[1,2,256,6]{2,3,1,0:T(8,128)S(1)}, u32[]{:S(2)}, u32[]{:S(2)}) collective-permute-start(f32[1,2,256,6]{2,3,1,0:T(8,128)S(1)} %get-tuple-element.234), channel_id=1, source_target_pairs={{1,0},{2,1},{3,2},{4,3},{5,4},{6,5},{7,6},{8,7},{9,8},{10,9},{11,1... | collective-permute-start | bytes 36872 | tf_op jit(solution)/shard_map/ppermute | solution.py:30
  637.4 15.8 %collective-permute-start.35 = (f32[1,2,128,6]{2,3,1,0:T(8,128)S(1)}, f32[1,2,128,6]{2,3,1,0:T(8,128)S(1)}, u32[]{:S(2)}, u32[]{:S(2)}) collective-permute-start(f32[1,2,128,6]{2,3,1,0:T(8,128)S(1)} %get-tuple-element.294), channel_id=1, source_target_pairs={{1,0},{2,1},{3,2},{4,3},{5,4},{6,5},{7,6},{8,7},{9,8},{10,9},{11,1... | collective-permute-start | bytes 18440 | tf_op jit(solution)/shard_map/ppermute | solution.py:30
  676.6 15.2 %all-to-all-start.6 = ((f32[32,1,128]{2,1,0:T(1,128)}), f32[32,1,128]{2,1,0:T(1,128)S(1)}, u32[]{:S(2)}, u32[]{:S(2)}) async-start(f32[32,1,128]{2,1,0:T(1,128)} %reshape.114), calls=%async_computation.6 | async-start | bytes 32768 | tf_op jit(solution)/shard_map/all_to_all | solution.py:133
  694.0 11.3 %collective-permute-start.36 = (f32[4,2,64,3]{3,2,1,0:T(8,128)}, f32[4,2,64,3]{3,2,1,0:T(8,128)S(1)}, u32[]{:S(2)}, u32[]{:S(2)}) collective-permute-start(f32[4,2,64,3]{3,2,1,0:T(8,128)} %get-tuple-element.187), channel_id=1, source_target_pairs={{0,1},{1,2},{2,3},{3,4},{4,5},{5,6},{6,7},{7,8},{8,9},{9,10},{10,1... | collective-permute-start | bytes 18440 | tf_op jit(solution)/shard_map/ppermute | solution.py:27
  698.6 22.0 %collective-permute-start.37 = (f32[4,2,64,3]{3,2,1,0:T(8,128)}, f32[4,2,64,3]{3,2,1,0:T(8,128)S(1)}, u32[]{:S(2)}, u32[]{:S(2)}) collective-permute-start(f32[4,2,64,3]{3,2,1,0:T(8,128)} %get-tuple-element.188), channel_id=1, source_target_pairs={{1,0},{2,1},{3,2},{4,3},{5,4},{6,5},{7,6},{8,7},{9,8},{10,9},{11,1... | collective-permute-start | bytes 18440 | tf_op jit(solution)/shard_map/ppermute | solution.py:30
  723.3 15.9 %collective-permute-start.39 = (f32[4,2,128,3]{2,3,1,0:T(4,128)S(1)}, f32[4,2,128,3]{2,3,1,0:T(4,128)S(1)}, u32[]{:S(2)}, u32[]{:S(2)}) collective-permute-start(f32[4,2,128,3]{2,3,1,0:T(4,128)S(1)} %get-tuple-element.231), channel_id=1, source_target_pairs={{1,0},{2,1},{3,2},{4,3},{5,4},{6,5},{7,6},{8,7},{9,8},{10,9},{11,1... | collective-permute-start | bytes 36872 | tf_op jit(solution)/shard_map/ppermute | solution.py:30
  741.9 19.6 %all-to-all-start.7 = ((f32[32,1,512]{2,1,0:T(1,128)}), f32[32,1,512]{2,1,0:T(1,128)S(1)}, u32[]{:S(2)}, u32[]{:S(2)}) async-start(f32[32,1,512]{2,1,0:T(1,128)} %reshape.116), calls=%async_computation.7 | async-start | bytes 131072 | tf_op jit(solution)/shard_map/all_to_all | solution.py:137
  763.8 34.8 %collective-permute-start.40 = (f32[4,64,3,32]{3,1,2,0:T(8,128)}, f32[4,64,3,32]{3,1,2,0:T(8,128)}, u32[]{:S(2)}, u32[]{:S(2)}) collective-permute-start(f32[4,64,3,32]{3,1,2,0:T(8,128)} %get-tuple-element.119), channel_id=1, source_target_pairs={{0,16},{16,32},{32,48},{48,64},{64,80},{80,96},{96,112},{112,128},... | collective-permute-start | bytes 294920 | tf_op jit(solution)/shard_map/ppermute | solution.py:27
  766.0 32.6 %collective-permute-start.41 = (f32[4,64,3,32]{3,1,2,0:T(8,128)}, f32[4,64,3,32]{3,1,2,0:T(8,128)}, u32[]{:S(2)}, u32[]{:S(2)}) collective-permute-start(f32[4,64,3,32]{3,1,2,0:T(8,128)} %get-tuple-element.120), channel_id=1, source_target_pairs={{16,0},{32,16},{48,32},{64,48},{80,64},{96,80},{112,96},{128,112},... | collective-permute-start | bytes 294920 | tf_op jit(solution)/shard_map/ppermute | solution.py:30
  804.7 10.3 collective-permute-start.42
  811.3 16.9 %collective-permute-start.43 = (f32[4,64,14,3]{1,0,3,2:T(4,128)}, f32[4,64,14,3]{1,0,3,2:T(4,128)}, u32[]{:S(2)}, u32[]{:S(2)}) collective-permute-start(f32[4,64,14,3]{1,0,3,2:T(4,128)} %copy.766), channel_id=1, source_target_pairs={{1,0},{2,1},{3,2},{4,3},{5,4},{6,5},{7,6},{8,7},{9,8},{10,9},{11,1... | collective-permute-start | bytes 129032 | tf_op jit(solution)/shard_map/ppermute | solution.py:30
  847.2 115.4 %collective-permute-start.44 = (f32[4,64,3,64]{3,1,2,0:T(8,128)}, f32[4,64,3,64]{3,1,2,0:T(8,128)}, u32[]{:S(2)}, u32[]{:S(2)}) collective-permute-start(f32[4,64,3,64]{3,1,2,0:T(8,128)} %get-tuple-element.71), channel_id=1, source_target_pairs={{0,16},{16,32},{32,48},{48,64},{64,80},{80,96},{96,112},{112,128},... | collective-permute-start | bytes 589832 | tf_op jit(solution)/shard_map/ppermute | solution.py:27
  849.1 113.5 %collective-permute-start.45 = (f32[4,64,3,64]{3,1,2,0:T(8,128)}, f32[4,64,3,64]{3,1,2,0:T(8,128)}, u32[]{:S(2)}, u32[]{:S(2)}) collective-permute-start(f32[4,64,3,64]{3,1,2,0:T(8,128)} %get-tuple-element.72), channel_id=1, source_target_pairs={{16,0},{32,16},{48,32},{64,48},{80,64},{96,80},{112,96},{128,112},... | collective-permute-start | bytes 589832 | tf_op jit(solution)/shard_map/ppermute | solution.py:30
  970.2 14.6 %collective-permute-start.46 = (f32[4,64,22,3]{1,0,3,2:T(4,128)S(1)}, f32[4,64,22,3]{1,0,3,2:T(4,128)S(1)}, u32[]{:S(2)}, u32[]{:S(2)}) collective-permute-start(f32[4,64,22,3]{1,0,3,2:T(4,128)S(1)} %copy.772), channel_id=1, source_target_pairs={{0,1},{1,2},{2,3},{3,4},{4,5},{5,6},{6,7},{7,8},{8,9},{9,10},{10,1... | collective-permute-start | bytes 202760 | tf_op jit(solution)/shard_map/ppermute | solution.py:27
  980.8 21.7 %collective-permute-start.47 = (f32[4,64,22,3]{1,0,3,2:T(4,128)}, f32[4,64,22,3]{1,0,3,2:T(4,128)}, u32[]{:S(2)}, u32[]{:S(2)}) collective-permute-start(f32[4,64,22,3]{1,0,3,2:T(4,128)} %copy.773), channel_id=1, source_target_pairs={{1,0},{2,1},{3,2},{4,3},{5,4},{6,5},{7,6},{8,7},{9,8},{10,9},{11,1... | collective-permute-start | bytes 202760 | tf_op jit(solution)/shard_map/ppermute | solution.py:30
  (45 other events, 1390.5 us)
where the time goes:
time: 1050 us; the launch traced here: 1030 us
  waiting for transfers between devices  278 us (26%)
  local copies, waits for them, and re-layouts  240 us (23%)
  starting transfers between devices  240 us (23%)
  blocking collectives  178 us (17%)
  other arithmetic  86.4 us (8%)
    ppermute x24, waiting for transfers between devices, extended_2(): lax.ppermute(lax.slice_in_dim(block, 0, width, axis=dim), axis, backward)  223 us
    ppermute x24, starting transfers between devices, extended_2(): lax.ppermute(lax.slice_in_dim(block, 0, width, axis=dim), axis, backward)  135 us
    psum x1, blocking collectives, body(): grad_point, grad_bias = lax.psum((point_term, bias_term), ('lat', 'lon'))  99.6 us
    ppermute x24, starting transfers between devices, extended_2(): lax.ppermute(lax.slice_in_dim(block, block.shape[dim] - width, None, axis...  82.4 us
    slice x20, local copies, waits for them, and re-layouts, split_axis(): odds = lax.slice_in_dim(extended, 1, span, 2, axis)  55.4 us
    slice x24, local copies, waits for them, and re-layouts, split_axis(): evens = lax.slice_in_dim(extended, 0, span, 2, axis)  55.1 us
    all_to_all x2, blocking collectives, descend(): lax.all_to_all(approx, 'lat', split_axis=0, concat_axis=1, tiled=True)  48.2 us
    slice x26, local copies, waits for them, and re-layouts, extended_2(): lax.slice_in_dim(block, block.shape[dim] - width, None, axis=dim)  34.4 us
  transfers between devices with their start and end apart: 52, of which 31 were waited for; matrix products, arithmetic and copies ran while one was open for 8% of the time, Pallas kernels for 0%

commit v1 on v0

v1 whole, which is shorter than its diff:
```python
import math

import numpy as np

import jax
import jax.numpy as jnp
from jax import lax
from jax.experimental import pallas as pl
from jax.experimental.pallas import tpu as pltpu
from jax.sharding import PartitionSpec as P

LOW = np.array(
    [
        0.23037781330885523,
        0.7148465705525415,
        0.6308807679295904,
        -0.02798376941698385,
        -0.18703481171888114,
        0.030841381835986965,
        0.032883011666982945,
        -0.010597401784997278,
    ],
    np.float64,
)
HIGH = np.array([LOW[7 - j] if j % 2 == 0 else -LOW[7 - j] for j in range(8)])

C = 64
H = 32
W = 128
LAT = 32
LON = 16
PAIRS = H // 2
F32 = jnp.float32
BF16 = jnp.bfloat16
MESH = pl.DeviceIdType.MESH


def long_filters():
    def spread(taps, step):
        out = np.zeros((len(taps) - 1) * step + 1)
        out[::step] = taps
        return out

    third = np.ones(1)
    for level in range(3):
        third = np.convolve(third, spread(LOW, 2**level))
    return [np.convolve(third, spread(LOW, 8)), np.convolve(third, spread(HIGH, 8))]


def tap(taps, at):
    return taps[at] if 0 <= at < len(taps) else 0.0


def tables():
    both = long_filters()
    lat = np.zeros((PAIRS, 4, 2, 2, 2, C))
    for h2 in range(PAIRS):
        for dl in range(4):
            for u in range(2):
                for ii in range(2):
                    for p in range(2):
                        lat[h2, dl, u, ii, p, :] = tap(both[u], 2 * h2 + p + 32 * dl - 16 * ii)
    lat = lat.reshape(PAIRS * 16, 2 * C).astype(np.float32)
    lon = np.zeros((2, 2, 8, W))
    for ds in range(2):
        for v in range(2):
            for jj in range(8):
                for w in range(W):
                    lon[ds, v, jj, w] = tap(both[v], w + 128 * ds - 16 * jj)
    lon = lon.reshape(32, W).astype(np.float32)
    high = lon.astype(jnp.bfloat16).astype(np.float32)
    rest = (lon - high).astype(jnp.bfloat16).astype(np.float32)
    split = np.concatenate(
        [np.concatenate([high, high], 1), np.concatenate([rest, np.zeros_like(rest)], 1)], 0
    )
    join = np.concatenate([high, rest, high], 0)
    return lat, split, join


def halves(x):
    high = x.astype(BF16)
    return high, (x - high.astype(F32)).astype(BF16)


def swap(x):
    return pltpu.roll(x, 64, axis=1)


def dot_nt(a, b):
    return lax.dot_general(a, b, (((1,), (1,)), ((), ())), preferred_element_type=F32)


def dot_tn(a, b):
    return lax.dot_general(a, b, (((0,), (0,)), ((), ())), preferred_element_type=F32)


def gelu_slope(p):
    cdf = 0.5 * (1.0 + lax.erf(p * (1.0 / math.sqrt(2.0))))
    pdf = jnp.exp(-0.5 * p * p) * (1.0 / math.sqrt(2.0 * math.pi))
    return cdf + p * pdf


def kernel(
    field, cot, wa, wd, wpoint, bias, lat_hbm, split_hbm, join_hbm,
    out_field, out_ga, out_gd, out_gp, out_gb,
    fbuf, cbuf, wbuf, wpbuf, biasbuf, lat_tab, split_tab, join_tab,
    wfwd, wbwd, base, grad, thl, ghl, yscr, dup,
    send1, send2, send3, send4, recv1, recv2, recv3, recv4, coarse,
    gwbuf, obuf, gpbuf, gbbuf, red1, red2, red3, red4,
    load_sem, fload_sem, store_sem, ostore_sem, send_sem, recv_sem, rsend_sem, rrecv_sem,
):
    lat_at = lax.axis_index("lat")
    lon_at = lax.axis_index("lon")
    left = lax.broadcasted_iota(jnp.int32, (32, 2 * C), 1) < C

    steps = [(dl, ds) for dl in (3, 2, 1, 0) for ds in (1, 0) if (dl, ds) != (0, 0)]
    behind = [(lax.rem(lat_at + (LAT - dl), LAT), lax.rem(lon_at + (LON - ds), LON)) for dl, ds in steps]
    ahead = [(lax.rem(lat_at + dl, LAT), lax.rem(lon_at + ds, LON)) for dl, ds in steps]
    k_at = lax.rem(lon_at, 8)
    zhi = lon_at // 8
    y_at = lax.rem(lat_at, 4)
    zlo = lat_at // 4
    q_at = zhi * 4 + y_at
    k_peers = [lax.rem(k_at + d, 8) for d in range(1, 8)]
    q_peers = [lax.rem(q_at + d, 8) for d in range(1, 8)]
    z_peers = [lax.rem(zlo + d, 8) for d in range(1, 8)]
    k_ids = [(lat_at, zhi * 8 + k) for k in k_peers]
    q_ids = [(zlo * 4 + lax.rem(q, 4), (q // 4) * 8 + k_at) for q in q_peers]
    z_ids = [(z * 4 + y_at, lon_at) for z in z_peers]

    barrier = pltpu.get_barrier_semaphore()
    everyone = behind + ahead + k_ids + q_ids + z_ids

    field_loads = [
        pltpu.make_async_copy(field.at[:, pl.ds(8 * q, 8), :], fbuf.at[q], fload_sem.at[q]) for q in range(4)
    ]
    for load in field_loads:
        load.start()
    split_load = pltpu.make_async_copy(split_hbm, split_tab, load_sem.at[0])
    lat_load = pltpu.make_async_copy(lat_hbm, lat_tab, load_sem.at[1])
    wp_load = pltpu.make_async_copy(wpoint, wpbuf, load_sem.at[2])
    bias_load = pltpu.make_async_copy(bias, biasbuf, load_sem.at[3])
    wa_load = pltpu.make_async_copy(wa, wbuf.at[0], load_sem.at[4])
    wd_load = pltpu.make_async_copy(wd, wbuf.at[pl.ds(1, 3)], load_sem.at[5])
    cot_loads = [
        pltpu.make_async_copy(cot.at[:, pl.ds(8 * q, 8), :], cbuf.at[q], fload_sem.at[4 + q]) for q in range(4)
    ]
    join_load = pltpu.make_async_copy(join_hbm, join_tab, load_sem.at[6])
    for load in [split_load, lat_load, wp_load, bias_load, wa_load, wd_load, join_load] + cot_loads:
        load.start()
    for device in everyone:
        pl.semaphore_signal(barrier, inc=1, device_id=device, device_id_type=MESH)

    def cell_pair(buffer, h2):
        chunk, row = h2 // 4, (h2 % 4) * 2
        flat = buffer.at[chunk].reshape(C * 8, W)
        return jnp.concatenate([flat[pl.ds(row + p, C, stride=8), :] for p in range(2)], 0)

    def lon_split(rows, at):
        both = dot_nt(split_tab[...].astype(BF16), rows)
        sums = both[:32] + both[32:]
        yscr[at, :, :] = sums[:, :128]
        yscr[at + 1, :, :] = sums[:, 128:]

    def lat_split(buffer, on_block):
        for dl in (3, 2, 1, 0):
            def step(g, sums, dl=dl):
                sums = list(sums)
                for n in range(4):
                    h2 = g * 4 + n
                    y = yscr[h2]
                    for m in range(4):
                        sums[m] = sums[m] + lat_tab[pl.ds(h2 * 16 + dl * 4 + m, 1), :] * y
                return tuple(sums)

            zero = jnp.zeros((32, 2 * C), F32)
            sums = lax.fori_loop(0, 4, step, (zero,) * 4)
            for u in range(2):
                first, second = sums[2 * u], sums[2 * u + 1]
                modes = jnp.where(left, first, second) + swap(jnp.where(left, second, first))
                for ds in range(2):
                    buffer[dl * 2 + ds, u * 16:(u + 1) * 16, :] = modes[ds * 16:(ds + 1) * 16]
            on_block(dl)

    def exchange(number, source_of, recv, targets):
        return [
            pltpu.make_async_remote_copy(
                src_ref=source_of(dl * 2 + ds),
                dst_ref=recv.at[dl * 2 + ds],
                send_sem=send_sem.at[number, n],
                recv_sem=recv_sem.at[number, n],
                device_id=targets[n],
                device_id_type=MESH,
            )
            for n, (dl, ds) in enumerate(steps)
        ]

    def start_block(copies):
        def on_block(dl):
            for n, step in enumerate(steps):
                if step[0] == dl:
                    copies[n].start()
        return on_block

    def lat_join(recv, own):
        for dl in range(4):
            blocks = [own[...] if (dl, ds) == (0, 0) else recv[dl * 2 + ds] for ds in range(2)]
            for u in range(2):
                rows = jnp.concatenate([b[u * 16:(u + 1) * 16] for b in blocks], 0)
                turned = swap(rows)
                dup[dl * 4 + u * 2] = jnp.where(left, rows, turned)
                dup[dl * 4 + u * 2 + 1] = jnp.where(left, turned, rows)

    def lon_join(h2):
        total = jnp.zeros((32, 2 * C), F32)
        for m in range(16):
            total = total + lat_tab[pl.ds(h2 * 16 + m, 1), :] * dup[m]
        high, rest = halves(total)
        return dot_tn(jnp.concatenate([high, high, rest], 0), join_tab[...].astype(BF16))

    def point_map(weights, rows):
        high = [rows[64 * n:64 * n + 64, :W] for n in range(4)]
        rest = [rows[64 * n:64 * n + 64, W:] for n in range(4)]
        high = jnp.concatenate(high, 1)
        rest = jnp.concatenate(rest, 1)
        out = dot_tn(weights, jnp.concatenate([high, rest, high], 0))
        return jnp.concatenate([out[:, W * n:W * n + W] for n in range(4)], 0)

    split_load.wait()
    for q in range(4):
        field_loads[q].wait()
        for n in range(2):
            h2 = q * 4 + n * 2
            for k in range(2):
                high, rest = halves(cell_pair(fbuf, h2 + k))
                thl[(h2 + k) * 128:(h2 + k + 1) * 128, :W] = high
                thl[(h2 + k) * 128:(h2 + k + 1) * 128, W:] = rest
            lon_split(thl[h2 * 128:h2 * 128 + 256, :], h2)
    lat_load.wait()
    pl.semaphore_wait(barrier, len(everyone))
    copies1 = exchange(0, lambda n: send1.at[n], recv1, behind)
    lat_split(send1, start_block(copies1))

    wp_load.wait()
    bias_load.wait()
    high, rest = halves(wpbuf[...])
    wbwd[...] = jnp.concatenate([high, high, rest], 0)
    high, rest = halves(wpbuf[...].T)
    wfwd[...] = jnp.concatenate([high, high, rest], 0)
    bias_cells = jnp.broadcast_to(biasbuf[...], (W, C)).T
    bias_cells = jnp.concatenate([bias_cells, bias_cells], 0)
    for h4 in range(PAIRS // 2):
        mapped = point_map(wfwd[...], thl[h4 * 256:h4 * 256 + 256, :])
        for k in range(2):
            h2 = 2 * h4 + k
            base[h2] = mapped[128 * k:128 * k + 128] + cell_pair(fbuf, h2) + bias_cells
    wa_load.wait()
    wd_load.wait()

    total = send1[0]
    for n, (dl, ds) in enumerate(steps):
        copies1[n].wait_recv()
        total = total + recv1[dl * 2 + ds]
    coarse[...] = total

    def mix(g, carry):
        turned, sums = carry
        sums = list(sums)
        for k in range(8):
            for b in range(4):
                rows = turned[8 * b:8 * b + 8]
                column = jnp.concatenate([rows[:, k:k + 1], rows[:, C + k:C + k + 1]], 0)
                sums[b] = sums[b] + column * wbuf[b, g * 8 + k]
        return pltpu.roll(turned, 2 * C - 8, axis=1), tuple(sums)

    def packed(parts):
        return jnp.concatenate([jnp.concatenate([p[:8], p[8:]], 1) for p in parts], 0)

    _, mixed = lax.fori_loop(0, C // 8, mix, (total, (jnp.zeros((16, C), F32),) * 4))
    send2[...] = packed(mixed) - total
    copies2 = exchange(1, lambda n: send2, recv2, ahead)
    for copy in copies2:
        copy.start()

    join_load.wait()
    for load in cot_loads:
        load.wait()
    for copy in copies2:
        copy.wait_recv()
    lat_join(recv2, send2)

    for h4 in range(PAIRS // 2):
        for k in range(2):
            h2 = 2 * h4 + k
            g = gelu_slope(base[h2] + lon_join(h2)) * cell_pair(cbuf, h2)
            grad[h2] = g
            high, rest = halves(g)
            ghl[h2 * 128:(h2 + 1) * 128, :W] = high
            ghl[h2 * 128:(h2 + 1) * 128, W:] = rest
        lon_split(ghl[h4 * 256:h4 * 256 + 256, :], 2 * h4)
    copies3 = exchange(2, lambda n: send3.at[n], recv3, behind)
    lat_split(send3, start_block(copies3))

    point = jnp.zeros((128, 128), F32)
    rows_sum = jnp.zeros((C, W), F32)
    for h2 in range(PAIRS):
        at = h2 * 128
        both = []
        for source in (ghl, thl):
            tops = jnp.concatenate([source[at:at + 64, :W], source[at + 64:at + 128, :W]], 1)
            rests = jnp.concatenate([source[at:at + 64, W:], source[at + 64:at + 128, W:]], 1)
            both.append(jnp.concatenate([tops, rests], 0))
        point = point + dot_nt(both[0], both[1])
        rows_sum = rows_sum + grad[h2, 0:64, :] + grad[h2, 64:128, :]
    point = point[:C] + point[C:]
    point = point + swap(point)
    bias_term = jnp.sum(rows_sum, axis=1, keepdims=True)
    lane = lax.broadcasted_iota(jnp.int32, (C, 128), 1)
    gpbuf[...] = jnp.where(lane < C, point, jnp.where(lane == C, bias_term, 0.0))

    def reduce_copies(number, pairs, ids):
        return [
            pltpu.make_async_remote_copy(
                src_ref=src,
                dst_ref=dst,
                send_sem=rsend_sem.at[number, n],
                recv_sem=rrecv_sem.at[number, n],
                device_id=ids[n],
                device_id_type=MESH,
            )
            for n, (src, dst) in enumerate(pairs)
        ]

    def tile(ref, n):
        return ref.at[pl.ds(pl.multiple_of(8 * n, 8), 8)]

    def total8(ref):
        out = ref[0:8]
        for n in range(1, 8):
            out = out + ref[8 * n:8 * n + 8]
        return out

    red1[pl.ds(pl.multiple_of(8 * k_at, 8), 8), :] = gpbuf[pl.ds(pl.multiple_of(8 * k_at, 8), 8), :]
    reduce1 = reduce_copies(0, [(tile(gpbuf, k), tile(red1, k_at)) for k in k_peers], k_ids)
    for copy in reduce1:
        copy.start()

    for h4 in range(PAIRS // 2):
        mapped = point_map(wbwd[...], ghl[h4 * 256:h4 * 256 + 256, :])
        for k in range(2):
            h2 = 2 * h4 + k
            base[h2] = mapped[128 * k:128 * k + 128] + grad[h2]

    gtotal = send3[0]
    for n, (dl, ds) in enumerate(steps):
        copies3[n].wait_recv()
        gtotal = gtotal + recv3[dl * 2 + ds]

    def unpacked(rows, b):
        part = rows[8 * b:8 * b + 8]
        return jnp.concatenate([part[:, :C], part[:, C:]], 0)

    gmodes = [unpacked(gtotal, b) for b in range(4)]
    lanes16 = lax.broadcasted_iota(jnp.int32, (16, C), 1)

    def back(g, sums):
        sums = list(sums)
        for k in range(8):
            for b in range(4):
                one = jnp.sum(wbuf[b, g * 8 + k] * gmodes[b], axis=1, keepdims=True)
                sums[b] = jnp.where(lanes16 == g * 8 + k, one, sums[b])
        return tuple(sums)

    backs = lax.fori_loop(0, C // 8, back, (jnp.zeros((16, C), F32),) * 4)
    send4[...] = packed(backs) - gtotal
    copies4 = exchange(3, lambda n: send4, recv4, ahead)
    for copy in copies4:
        copy.start()

    for copy in reduce1:
        copy.wait_recv()
    red2[pl.ds(pl.multiple_of(8 * q_at, 8), 8), :] = total8(red1)
    reduce2 = reduce_copies(1, [(tile(red2, q_at), tile(red2, q_at))] * 7, q_ids)
    for copy in reduce2:
        copy.start()

    def outer(g, turned):
        for k in range(8):
            for b in range(4):
                rows = turned[8 * b:8 * b + 8]
                column = jnp.concatenate([rows[:, k:k + 1], rows[:, C + k:C + k + 1]], 0)
                gwbuf[b, g * 8 + k] = column * gmodes[b]
        return pltpu.roll(turned, 2 * C - 8, axis=1)

    lax.fori_loop(0, C // 8, outer, coarse[...])
    stores = [
        pltpu.make_async_copy(gwbuf.at[0], out_ga, store_sem.at[0]),
        pltpu.make_async_copy(gwbuf.at[pl.ds(1, 3)], out_gd, store_sem.at[1]),
    ]
    for store in stores:
        store.start()
    for copy in reduce2:
        copy.wait_recv()
    red3[pl.ds(pl.multiple_of(8 * zlo, 8), 8), :] = total8(red2)
    reduce3 = reduce_copies(2, [(tile(red3, zlo), tile(red3, zlo))] * 7, z_ids)
    for copy in reduce3:
        copy.start()

    for copy in copies4:
        copy.wait_recv()
    lat_join(recv4, send4)
    for h2 in range(PAIRS):
        cells = base[h2] + lon_join(h2)
        chunk, row = h2 // 4, (h2 % 4) * 2
        flat = obuf.at[chunk].reshape(C * 8, W)
        for p in range(2):
            flat[pl.ds(row + p, C, stride=8), :] = cells[64 * p:64 * p + 64]
        if h2 % 4 == 3:
            store = pltpu.make_async_copy(
                obuf.at[chunk], out_field.at[:, pl.ds(8 * chunk, 8), :], ostore_sem.at[chunk]
            )
            store.start()
            stores.append(store)
        if h2 == 7:
            for copy in reduce3:
                copy.wait_recv()
            red4[pl.ds(pl.multiple_of(8 * k_at, 8), 8), :] = total8(red3)
            reduce4 = reduce_copies(3, [(tile(red4, k_at), tile(red4, k_at))] * 7, k_ids)
            for copy in reduce4:
                copy.start()

    for copy in reduce4:
        copy.wait_recv()
    gpbuf2 = red4[...]
    gbbuf[...] = gpbuf2.T[C:C + 1, :]
    red_out = gpbuf2[:, :C]
    wpbuf[...] = red_out
    last = [
        pltpu.make_async_copy(wpbuf, out_gp, store_sem.at[2]),
        pltpu.make_async_copy(gbbuf, out_gb, store_sem.at[3]),
    ]
    for store in last:
        store.start()
    for store in stores + last:
        store.wait()
    for copy in copies1 + copies2 + copies3 + copies4 + reduce1 + reduce2 + reduce3 + reduce4:
        copy.wait_send()


def body(field, cotangent, w_approx, w_detail, w_point, bias):
    lat_tab, split_tab, join_tab = tables()
    wa = jnp.transpose(w_approx, (0, 2, 3, 1)).reshape(C, 16, C)
    wd = jnp.transpose(w_detail, (0, 1, 3, 4, 2)).reshape(3, C, 16, C)
    anywhere = pl.BlockSpec(memory_space=pl.ANY)
    vmem = pltpu.VMEM
    block = (32, 128)
    gfield, ga, gd, gp, gb = pl.pallas_call(
        kernel,
        out_shape=(
            jax.ShapeDtypeStruct((C, H, W), F32),
            jax.ShapeDtypeStruct((C, 16, C), F32),
            jax.ShapeDtypeStruct((3, C, 16, C), F32),
            jax.ShapeDtypeStruct((C, C), F32),
            jax.ShapeDtypeStruct((1, C), F32),
        ),
        in_specs=[anywhere] * 9,
        out_specs=(anywhere,) * 5,
        scratch_shapes=[
            vmem((4, C, 8, W), F32),
            vmem((4, C, 8, W), F32),
            vmem((4, C, 16, C), F32),
            vmem((C, C), F32),
            vmem((1, C), F32),
            vmem((PAIRS * 16, 2 * C), F32),
            vmem((64, 2 * W), F32),
            vmem((96, W), F32),
            vmem((3 * C, C), BF16),
            vmem((3 * C, C), BF16),
            vmem((PAIRS, 2 * C, W), F32),
            vmem((PAIRS, 2 * C, W), F32),
            vmem((PAIRS * 2 * C, 2 * W), BF16),
            vmem((PAIRS * 2 * C, 2 * W), BF16),
            vmem((PAIRS, 32, 2 * C), F32),
            vmem((16, 32, 2 * C), F32),
            vmem((8,) + block, F32),
            vmem(block, F32),
            vmem((8,) + block, F32),
            vmem(block, F32),
            vmem((8,) + block, F32),
            vmem((8,) + block, F32),
            vmem((8,) + block, F32),
            vmem((8,) + block, F32),
            vmem(block, F32),
            vmem((4, C, 16, C), F32),
            vmem((4, C, 8, W), F32),
            vmem((C, 128), F32),
            vmem((1, C), F32),
            vmem((C, 128), F32),
            vmem((C, 128), F32),
            vmem((C, 128), F32),
            vmem((C, 128), F32),
            pltpu.SemaphoreType.DMA((7,)),
            pltpu.SemaphoreType.DMA((8,)),
            pltpu.SemaphoreType.DMA((4,)),
            pltpu.SemaphoreType.DMA((4,)),
            pltpu.SemaphoreType.DMA((4, 7)),
            pltpu.SemaphoreType.DMA((4, 7)),
            pltpu.SemaphoreType.DMA((4, 7)),
            pltpu.SemaphoreType.DMA((4, 7)),
        ],
        compiler_params=pltpu.CompilerParams(
            collective_id=0, has_side_effects=True, vmem_limit_bytes=48 * 1024 * 1024
        ),
    )(
        field,
        cotangent,
        wa,
        wd,
        w_point,
        bias.reshape(1, C),
        jnp.asarray(lat_tab),
        jnp.asarray(split_tab),
        jnp.asarray(join_tab),
    )
    ga = jnp.transpose(ga.reshape(C, 2, 8, C), (0, 3, 1, 2))
    gd = jnp.transpose(gd.reshape(3, C, 2, 8, C), (0, 1, 4, 2, 3))
    return gfield, ga, gd, gp, gb.reshape(C)


def solution(mesh):
    placed = (
        P(None, "lat", "lon"),
        P(None, "lat", "lon"),
        P(None, None, "lat", "lon"),
        P(None, None, None, "lat", "lon"),
        P(),
        P(),
    )
    return jax.shard_map(
        body,
        mesh=mesh,
        in_specs=placed,
        out_specs=(
            P(None, "lat", "lon"),
            P(None, None, "lat", "lon"),
            P(None, None, None, "lat", "lon"),
            P(),
            P(),
        ),
        check_vma=False,
    )
```

time: 1050 us -> 87.9 us (0.08)
  the two profiles are of different devices: /device:TPU:7 before, /device:TPU:1 now
where the time goes in v1:
time: 87.9 us; the launch traced here: 87.5 us
  Pallas kernels  75.3 us (86%)
  local copies, waits for them, and re-layouts  11.5 us (13%)
    pallas_call x1, Pallas kernels, body(): pl.pallas_call(kernel, out_shape=(jax.ShapeDtypeStruct((C, H, W), F32), j...  75.3 us
    unnamed x21, local copies, waits for them, and re-layouts  11.5 us

profile of v1, /device:TPU:1, one launch (start us, length us, event | category | flops | bytes accessed | tf_op | source)
XLA Modules:
  0.0 87.5 jit_solution(4183828146575272143)
XLA Ops:
  0.6 0.0 copy-start
  0.6 1.2 %copy-done = f32[64,32,128]{2,1,0:T(8,128)S(1)} copy-done((f32[64,32,128]{2,1,0:T(8,128)S(1)}, f32[64,32,128]{2,1,0:T(8,128)}, u32[]{:S(2)}) %copy-start) | copy-done | bytes 1048600
  1.9 0.0 copy-start.1
  1.9 1.2 %copy-done.1 = f32[64,32,128]{2,1,0:T(8,128)S(1)} copy-done((f32[64,32,128]{2,1,0:T(8,128)S(1)}, f32[64,32,128]{2,1,0:T(8,128)}, u32[]{:S(2)}) %copy-start.1) | copy-done | bytes 1048600
  3.1 0.0 copy-start.2
  3.1 1.0 %copy-done.2 = f32[64,64,2,8]{1,3,2,0:T(8,128)S(1)} copy-done((f32[64,64,2,8]{1,3,2,0:T(8,128)S(1)}, f32[64,64,2,8]{1,3,2,0:T(8,128)}, u32[]{:S(2)}) %copy-start.2) | copy-done | bytes 262168
  4.1 0.0 copy-start.3
  4.1 0.9 %copy-done.3 = f32[256,128]{1,0:T(8,128)S(1)} copy-done((f32[256,128]{1,0:T(8,128)S(1)}, f32[256,128]{1,0:T(8,128)}, u32[]{:S(2)}) %copy-start.3) | copy-done | bytes 131096
  5.0 0.0 copy-start.4
  5.0 0.8 copy-done.4
  5.9 0.0 copy-start.5
  5.9 0.8 copy-done.5
  6.7 0.0 copy-start.6
  6.7 0.8 copy-done.6
  7.4 0.0 copy-start.7
  7.4 0.7 copy-done.7
  8.1 75.3 %shard_map.128 = (f32[64,32,128]{2,1,0:T(8,128)S(1)}, f32[64,16,64]{2,1,0:T(8,128)S(1)}, f32[3,64,16,64]{3,2,1,0:T(8,128)S(1)}, f32[64,64]{1,0:T(8,128)S(1)}, f32[1,64]{1,0:T(1,128)S(1)}) custom-call(f32[64,32,128]{2,1,0:T(8,128)S(1)} %copy-done, f32[64,32,128]{2,1,0:T(8,128)S(1)} %copy-done.1, f32[64,16,64]{2,1,0:T(8,128)S(1)} %bitcast.15, ...), custom_call_target="tpu_custom_call" | custom-call | tf_op jit(solution)/shard_map/pallas_call | solution.py:457
  83.4 1.0 %copy.19 = f32[64,32,128]{2,1,0:T(8,128)} copy(f32[64,32,128]{2,1,0:T(8,128)S(1)} %get-tuple-element.20) | data formatting | bytes 2097152
  84.4 0.8 copy.20
  85.2 1.1 %copy.21 = f32[3,64,64,2,8]{2,4,3,1,0:T(8,128)} copy(f32[3,64,64,2,8]{2,4,3,1,0:T(8,128)S(1)} %bitcast.14) | data formatting | bytes 1572864
  86.3 0.6 copy.22
  87.0 0.5 copy.23
Async XLA Ops:
  0.6 1.2 %copy-start = (f32[64,32,128]{2,1,0:T(8,128)S(1)}, f32[64,32,128]{2,1,0:T(8,128)}, u32[]{:S(2)}) copy-start(f32[64,32,128]{2,1,0:T(8,128)} %field.1) | copy-start | bytes 3145732
  1.9 1.2 %copy-start.1 = (f32[64,32,128]{2,1,0:T(8,128)S(1)}, f32[64,32,128]{2,1,0:T(8,128)}, u32[]{:S(2)}) copy-start(f32[64,32,128]{2,1,0:T(8,128)} %cot.1) | copy-start | bytes 3145732
  3.1 1.0 %copy-start.2 = (f32[64,64,2,8]{1,3,2,0:T(8,128)S(1)}, f32[64,64,2,8]{1,3,2,0:T(8,128)}, u32[]{:S(2)}) copy-start(f32[64,64,2,8]{1,3,2,0:T(8,128)} %param.11) | copy-start | bytes 786436
  4.1 0.9 %copy-start.3 = (f32[256,128]{1,0:T(8,128)S(1)}, f32[256,128]{1,0:T(8,128)}, u32[]{:S(2)}) copy-start(f32[256,128]{1,0:T(8,128)} %constant.6.clone.lat_hbm) | copy-start | bytes 393220
  5.0 0.8 copy-start.4
  5.9 0.8 copy-start.5
  6.7 0.8 copy-start.6
  7.4 0.7 copy-start.7

commit v2 on v1

--- a/solution.py
+++ b/solution.py
@@ -100,36 +100,61 @@
     return cdf + p * pdf
 
 
+def lat_join(recv, own, dup, left):
+    for dl in range(4):
+        blocks = [own[...] if (dl, ds) == (0, 0) else recv[dl * 2 + ds] for ds in range(2)]
+        for u in range(2):
+            rows = jnp.concatenate([b[u * 16:(u + 1) * 16] for b in blocks], 0)
+            turned = swap(rows)
+            dup[dl * 4 + u * 2] = jnp.where(left, rows, turned)
+            dup[dl * 4 + u * 2 + 1] = jnp.where(left, turned, rows)
+
+
+def lon_join(h2, dup, lat_tab, join_tab):
+    total = jnp.zeros((32, 2 * C), F32)
+    for m in range(16):
+        total = total + lat_tab[pl.ds(h2 * 16 + m, 1), :] * dup[m]
+    high, rest = halves(total)
+    return dot_tn(jnp.concatenate([high, high, rest], 0), join_tab[...].astype(BF16))
+
+
 def kernel(
     field, cot, wa, wd, wpoint, bias, lat_hbm, split_hbm, join_hbm,
-    out_field, out_ga, out_gd, out_gp, out_gb,
-    fbuf, cbuf, wbuf, wpbuf, biasbuf, lat_tab, split_tab, join_tab,
-    wfwd, wbwd, base, grad, thl, ghl, yscr, dup,
-    send1, send2, send3, send4, recv1, recv2, recv3, recv4, coarse,
-    gwbuf, obuf, gpbuf, gbbuf, red1, red2, red3, red4,
-    load_sem, fload_sem, store_sem, ostore_sem, send_sem, recv_sem, rsend_sem, rrecv_sem,
+    base, recv4, send4, out_gw, out_gp, out_gb, lat_tab, join_tab,
+    fbuf, cbuf, wbuf, wpbuf, biasbuf, split_tab,
+    wfwd, wbwd, grad, thl, ghl, yscr, dup,
+    send1, send2, send3, recv1, recv2, recv3, coarse,
+    red1, red2, red3, red4, red5,
+    load_sem, fload_sem, send_sem, recv_sem, rsend_sem, rrecv_sem,
 ):
     lat_at = lax.axis_index("lat")
     lon_at = lax.axis_index("lon")
     left = lax.broadcasted_iota(jnp.int32, (32, 2 * C), 1) < C
 
-    steps = [(dl, ds) for dl in (3, 2, 1, 0) for ds in (1, 0) if (dl, ds) != (0, 0)]
+    steps = [(0, 1), (1, 1), (2, 1), (3, 1), (3, 0), (2, 0), (1, 0)]
     behind = [(lax.rem(lat_at + (LAT - dl), LAT), lax.rem(lon_at + (LON - ds), LON)) for dl, ds in steps]
     ahead = [(lax.rem(lat_at + dl, LAT), lax.rem(lon_at + ds, LON)) for dl, ds in steps]
-    k_at = lax.rem(lon_at, 8)
     zhi = lon_at // 8
+    x_at = lax.rem(lon_at, 8) // 2
+    core = lax.rem(lon_at, 2)
     y_at = lax.rem(lat_at, 4)
     zlo = lat_at // 4
-    q_at = zhi * 4 + y_at
-    k_peers = [lax.rem(k_at + d, 8) for d in range(1, 8)]
-    q_peers = [lax.rem(q_at + d, 8) for d in range(1, 8)]
-    z_peers = [lax.rem(zlo + d, 8) for d in range(1, 8)]
-    k_ids = [(lat_at, zhi * 8 + k) for k in k_peers]
-    q_ids = [(zlo * 4 + lax.rem(q, 4), (q // 4) * 8 + k_at) for q in q_peers]
-    z_ids = [(z * 4 + y_at, lon_at) for z in z_peers]
+    run, inner = zhi * 2 + zlo // 4, lax.rem(zlo, 4)
+
+    def at(z_run, z_inner):
+        return (lax.rem(z_run, 2) * 16 + z_inner * 4 + y_at, (z_run // 2) * 8 + lax.rem(lon_at, 8))
+
+    turns = [lambda i, d=d: lax.rem(i + d, 4) for d in (2, 1, 3)]
+    sum_steps = [
+        (core, [(lat_at, lon_at + 1 - 2 * core)]),
+        (y_at, [(zlo * 4 + t(y_at), lon_at) for t in turns]),
+        (x_at, [(lat_at, zhi * 8 + t(x_at) * 2 + core) for t in turns]),
+        (inner, [at(run, t(inner)) for t in turns]),
+        (run, [at(t(run), inner) for t in turns]),
+    ]
 
     barrier = pltpu.get_barrier_semaphore()
-    everyone = behind + ahead + k_ids + q_ids + z_ids
+    everyone = sum_steps[4][1] + behind + ahead + sum_steps[3][1] + sum_steps[2][1]
 
     field_loads = [
         pltpu.make_async_copy(field.at[:, pl.ds(8 * q, 8), :], fbuf.at[q], fload_sem.at[q]) for q in range(4)
@@ -202,22 +227,6 @@
                     copies[n].start()
         return on_block
 
-    def lat_join(recv, own):
-        for dl in range(4):
-            blocks = [own[...] if (dl, ds) == (0, 0) else recv[dl * 2 + ds] for ds in range(2)]
-            for u in range(2):
-                rows = jnp.concatenate([b[u * 16:(u + 1) * 16] for b in blocks], 0)
-                turned = swap(rows)
-                dup[dl * 4 + u * 2] = jnp.where(left, rows, turned)
-                dup[dl * 4 + u * 2 + 1] = jnp.where(left, turned, rows)
-
-    def lon_join(h2):
-        total = jnp.zeros((32, 2 * C), F32)
-        for m in range(16):
-            total = total + lat_tab[pl.ds(h2 * 16 + m, 1), :] * dup[m]
-        high, rest = halves(total)
-        return dot_tn(jnp.concatenate([high, high, rest], 0), join_tab[...].astype(BF16))
-
     def point_map(weights, rows):
         high = [rows[64 * n:64 * n + 64, :W] for n in range(4)]
         rest = [rows[64 * n:64 * n + 64, W:] for n in range(4)]
@@ -287,12 +296,12 @@
         load.wait()
     for copy in copies2:
         copy.wait_recv()
-    lat_join(recv2, send2)
+    lat_join(recv2, send2, dup, left)
 
     for h4 in range(PAIRS // 2):
         for k in range(2):
             h2 = 2 * h4 + k
-            g = gelu_slope(base[h2] + lon_join(h2)) * cell_pair(cbuf, h2)
+            g = gelu_slope(base[h2] + lon_join(h2, dup, lat_tab, join_tab)) * cell_pair(cbuf, h2)
             grad[h2] = g
             high, rest = halves(g)
             ghl[h2 * 128:(h2 + 1) * 128, :W] = high
@@ -315,41 +324,50 @@
     point = point[:C] + point[C:]
     point = point + swap(point)
     bias_term = jnp.sum(rows_sum, axis=1, keepdims=True)
-    lane = lax.broadcasted_iota(jnp.int32, (C, 128), 1)
-    gpbuf[...] = jnp.where(lane < C, point, jnp.where(lane == C, bias_term, 0.0))
-
-    def reduce_copies(number, pairs, ids):
-        return [
+    sums_of = [red1, red2, red3, red4, red5]
+    folded = jnp.concatenate([point[: C // 2, :C], point[C // 2:, :C]], 1)
+    bias_row = jnp.broadcast_to(bias_term, (C, 128)).T[:8]
+    first = jnp.concatenate([folded, jnp.concatenate([bias_row, bias_row], 1)], 0)
+    reduces = []
+
+    def send_sum(number, rows):
+        own, ids = sum_steps[number]
+        ref = sums_of[number]
+        ref[pl.ds(own, 1)] = rows[None]
+        copies = [
             pltpu.make_async_remote_copy(
-                src_ref=src,
-                dst_ref=dst,
+                src_ref=ref.at[own],
+                dst_ref=ref.at[own],
                 send_sem=rsend_sem.at[number, n],
                 recv_sem=rrecv_sem.at[number, n],
-                device_id=ids[n],
+                device_id=device,
                 device_id_type=MESH,
             )
-            for n, (src, dst) in enumerate(pairs)
+            for n, device in enumerate(ids)
         ]
-
-    def tile(ref, n):
-        return ref.at[pl.ds(pl.multiple_of(8 * n, 8), 8)]
-
-    def total8(ref):
-        out = ref[0:8]
-        for n in range(1, 8):
-            out = out + ref[8 * n:8 * n + 8]
-        return out
-
-    red1[pl.ds(pl.multiple_of(8 * k_at, 8), 8), :] = gpbuf[pl.ds(pl.multiple_of(8 * k_at, 8), 8), :]
-    reduce1 = reduce_copies(0, [(tile(gpbuf, k), tile(red1, k_at)) for k in k_peers], k_ids)
-    for copy in reduce1:
-        copy.start()
+        for copy in copies:
+            copy.start()
+        reduces.append(copies)
+
+    def take_sum(number):
+        for copy in reduces[number]:
+            copy.wait_recv()
+        ref = sums_of[number]
+        rows = ref[0]
+        for n in range(1, len(reduces[number]) + 1):
+            rows = rows + ref[n]
+        return rows
+
+    send_sum(0, first)
 
     for h4 in range(PAIRS // 2):
         mapped = point_map(wbwd[...], ghl[h4 * 256:h4 * 256 + 256, :])
         for k in range(2):
             h2 = 2 * h4 + k
             base[h2] = mapped[128 * k:128 * k + 128] + grad[h2]
+    send_sum(1, take_sum(0))
+    send_sum(2, take_sum(1))
+    send_sum(3, take_sum(2))
 
     gtotal = send3[0]
     for n, (dl, ds) in enumerate(steps):
@@ -377,74 +395,52 @@
     for copy in copies4:
         copy.start()
 
-    for copy in reduce1:
-        copy.wait_recv()
-    red2[pl.ds(pl.multiple_of(8 * q_at, 8), 8), :] = total8(red1)
-    reduce2 = reduce_copies(1, [(tile(red2, q_at), tile(red2, q_at))] * 7, q_ids)
-    for copy in reduce2:
-        copy.start()
+    send_sum(4, take_sum(3))
 
     def outer(g, turned):
         for k in range(8):
             for b in range(4):
                 rows = turned[8 * b:8 * b + 8]
                 column = jnp.concatenate([rows[:, k:k + 1], rows[:, C + k:C + k + 1]], 0)
-                gwbuf[b, g * 8 + k] = column * gmodes[b]
+                out_gw[b, g * 8 + k] = column * gmodes[b]
         return pltpu.roll(turned, 2 * C - 8, axis=1)
 
     lax.fori_loop(0, C // 8, outer, coarse[...])
-    stores = [
-        pltpu.make_async_copy(gwbuf.at[0], out_ga, store_sem.at[0]),
-        pltpu.make_async_copy(gwbuf.at[pl.ds(1, 3)], out_gd, store_sem.at[1]),
-    ]
-    for store in stores:
-        store.start()
-    for copy in reduce2:
-        copy.wait_recv()
-    red3[pl.ds(pl.multiple_of(8 * zlo, 8), 8), :] = total8(red2)
-    reduce3 = reduce_copies(2, [(tile(red3, zlo), tile(red3, zlo))] * 7, z_ids)
-    for copy in reduce3:
-        copy.start()
-
     for copy in copies4:
         copy.wait_recv()
-    lat_join(recv4, send4)
+    rows = take_sum(4)
+    out_gp[...] = jnp.concatenate([rows[: C // 2, :C], rows[: C // 2, C:]], 0)
+    out_gb[...] = rows[C // 2:C // 2 + 1, :C]
+    for copy in copies1 + copies2 + copies3 + copies4 + sum(reduces, []):
+        copy.wait_send()
+
+
+def last_kernel(
+    base, recv4, send4, gw, gp, gb, lat_tab, join_tab, out_field, out_ga, out_gd, out_gp, out_gb, dup, obuf, sem
+):
+    stores = []
+
+    def store(src, dst):
+        stores.append(pltpu.make_async_copy(src, dst, sem.at[len(stores)]))
+        stores[-1].start()
+
+    store(gw.at[0], out_ga)
+    for b in range(3):
+        store(gw.at[1 + b], out_gd.at[b])
+    store(gp, out_gp)
+    store(gb, out_gb)
+    left = lax.broadcasted_iota(jnp.int32, (32, 2 * C), 1) < C
+    lat_join(recv4, send4, dup, left)
     for h2 in range(PAIRS):
-        cells = base[h2] + lon_join(h2)
+        cells = base[h2] + lon_join(h2, dup, lat_tab, join_tab)
         chunk, row = h2 // 4, (h2 % 4) * 2
         flat = obuf.at[chunk].reshape(C * 8, W)
         for p in range(2):
             flat[pl.ds(row + p, C, stride=8), :] = cells[64 * p:64 * p + 64]
         if h2 % 4 == 3:
-            store = pltpu.make_async_copy(
-                obuf.at[chunk], out_field.at[:, pl.ds(8 * chunk, 8), :], ostore_sem.at[chunk]
-            )
-            store.start()
-            stores.append(store)
-        if h2 == 7:
-            for copy in reduce3:
-                copy.wait_recv()
-            red4[pl.ds(pl.multiple_of(8 * k_at, 8), 8), :] = total8(red3)
-            reduce4 = reduce_copies(3, [(tile(red4, k_at), tile(red4, k_at))] * 7, k_ids)
-            for copy in reduce4:
-                copy.start()
-
-    for copy in reduce4:
-        copy.wait_recv()
-    gpbuf2 = red4[...]
-    gbbuf[...] = gpbuf2.T[C:C + 1, :]
-    red_out = gpbuf2[:, :C]
-    wpbuf[...] = red_out
-    last = [
-        pltpu.make_async_copy(wpbuf, out_gp, store_sem.at[2]),
-        pltpu.make_async_copy(gbbuf, out_gb, store_sem.at[3]),
-    ]
-    for store in last:
-        store.start()
-    for store in stores + last:
-        store.wait()
-    for copy in copies1 + copies2 + copies3 + copies4 + reduce1 + reduce2 + reduce3 + reduce4:
-        copy.wait_send()
+            store(obuf.at[chunk], out_field.at[:, pl.ds(8 * chunk, 8), :])
+    for copy in stores:
+        copy.wait()
 
 
 def body(field, cotangent, w_approx, w_detail, w_point, bias):
@@ -454,29 +450,30 @@
     anywhere = pl.BlockSpec(memory_space=pl.ANY)
     vmem = pltpu.VMEM
     block = (32, 128)
-    gfield, ga, gd, gp, gb = pl.pallas_call(
+    hbm = pl.BlockSpec(memory_space=pltpu.HBM)
+    results = pl.pallas_call(
         kernel,
         out_shape=(
-            jax.ShapeDtypeStruct((C, H, W), F32),
-            jax.ShapeDtypeStruct((C, 16, C), F32),
-            jax.ShapeDtypeStruct((3, C, 16, C), F32),
-            jax.ShapeDtypeStruct((C, C), F32),
-            jax.ShapeDtypeStruct((1, C), F32),
+            vmem((PAIRS, 2 * C, W), F32),
+            vmem((8,) + block, F32),
+            vmem(block, F32),
+            vmem((4, C, 16, C), F32),
+            vmem((C, C), F32),
+            vmem((1, C), F32),
+            vmem((PAIRS * 16, 2 * C), F32),
+            vmem((96, W), F32),
         ),
-        in_specs=[anywhere] * 9,
-        out_specs=(anywhere,) * 5,
+        in_specs=[hbm] * 9,
+        out_specs=(pl.BlockSpec(memory_space=vmem),) * 8,
         scratch_shapes=[
             vmem((4, C, 8, W), F32),
             vmem((4, C, 8, W), F32),
             vmem((4, C, 16, C), F32),
             vmem((C, C), F32),
             vmem((1, C), F32),
-            vmem((PAIRS * 16, 2 * C), F32),
             vmem((64, 2 * W), F32),
-            vmem((96, W), F32),
             vmem((3 * C, C), BF16),
             vmem((3 * C, C), BF16),
-            vmem((PAIRS, 2 * C, W), F32),
             vmem((PAIRS, 2 * C, W), F32),
             vmem((PAIRS * 2 * C, 2 * W), BF16),
             vmem((PAIRS * 2 * C, 2 * W), BF16),
@@ -485,43 +482,59 @@
             vmem((8,) + block, F32),
             vmem(block, F32),
             vmem((8,) + block, F32),
-            vmem(block, F32),
-            vmem((8,) + block, F32),
             vmem((8,) + block, F32),
             vmem((8,) + block, F32),
             vmem((8,) + block, F32),
             vmem(block, F32),
-            vmem((4, C, 16, C), F32),
-            vmem((4, C, 8, W), F32),
-            vmem((C, 128), F32),
-            vmem((1, C), F32),
-            vmem((C, 128), F32),
-            vmem((C, 128), F32),
-            vmem((C, 128), F32),
-            vmem((C, 128), F32),
+            vmem((2, 40, 128), F32),
+            vmem((4, 40, 128), F32),
+            vmem((4, 40, 128), F32),
+            vmem((4, 40, 128), F32),
+            vmem((4, 40, 128), F32),
             pltpu.SemaphoreType.DMA((7,)),
             pltpu.SemaphoreType.DMA((8,)),
-            pltpu.SemaphoreType.DMA((4,)),
-            pltpu.SemaphoreType.DMA((4,)),
             pltpu.SemaphoreType.DMA((4, 7)),
             pltpu.SemaphoreType.DMA((4, 7)),
-            pltpu.SemaphoreType.DMA((4, 7)),
-            pltpu.SemaphoreType.DMA((4, 7)),
+            pltpu.SemaphoreType.DMA((5, 3)),
+            pltpu.SemaphoreType.DMA((5, 3)),
         ],
         compiler_params=pltpu.CompilerParams(
             collective_id=0, has_side_effects=True, vmem_limit_bytes=48 * 1024 * 1024
         ),
     )(
-        field,
-        cotangent,
-        wa,
-        wd,
-        w_point,
-        bias.reshape(1, C),
-        jnp.asarray(lat_tab),
-        jnp.asarray(split_tab),
-        jnp.asarray(join_tab),
+        *[
+            pltpu.with_memory_space_constraint(x, pltpu.HBM)
+            for x in (
+                field,
+                cotangent,
+                wa,
+                wd,
+                w_point,
+                bias.reshape(1, C),
+                jnp.asarray(lat_tab),
+                jnp.asarray(split_tab),
+                jnp.asarray(join_tab),
+            )
+        ]
     )
+    gfield, ga, gd, gp, gb = pl.pallas_call(
+        last_kernel,
+        out_shape=(
+            jax.ShapeDtypeStruct((C, H, W), F32),
+            jax.ShapeDtypeStruct((C, 16, C), F32),
+            jax.ShapeDtypeStruct((3, C, 16, C), F32),
+            jax.ShapeDtypeStruct((C, C), F32),
+            jax.ShapeDtypeStruct((1, C), F32),
+        ),
+        in_specs=[pl.BlockSpec(memory_space=vmem)] * 8,
+        out_specs=(anywhere,) * 5,
+        scratch_shapes=[
+            vmem((16, 32, 2 * C), F32),
+            vmem((4, C, 8, W), F32),
+            pltpu.SemaphoreType.DMA((10,)),
+        ],
+        compiler_params=pltpu.CompilerParams(vmem_limit_bytes=32 * 1024 * 1024),
+    )(*[pltpu.with_memory_space_constraint(x, vmem) for x in results])
     ga = jnp.transpose(ga.reshape(C, 2, 8, C), (0, 3, 1, 2))
     gd = jnp.transpose(gd.reshape(3, C, 2, 8, C), (0, 1, 4, 2, 3))
     return gfield, ga, gd, gp, gb.reshape(C)

time: 87.9 us -> 68.5 us (0.78)
  the two profiles are of different devices: /device:TPU:1 before, /device:TPU:64 now
where the time goes in v2:
time: 68.5 us; the launch traced here: 68.4 us
  Pallas kernels  67.7 us (99%)
    pallas_call x1, Pallas kernels, body(): pl.pallas_call(kernel, out_shape=(vmem((PAIRS, 2 * C, W), F32), vmem((8,)...  66 us
    pallas_call x1, Pallas kernels, body(): pl.pallas_call(last_kernel, out_shape=(jax.ShapeDtypeStruct((C, H, W), F3...  1.76 us

profile of v2, /device:TPU:64, one launch (start us, length us, event | category | flops | bytes accessed | tf_op | source)
XLA Modules:
  0.0 68.4 jit_solution(827035643221937832)
XLA Ops:
  0.6 66.0 %shard_map.128 = (f32[16,128,128]{2,1,0:T(8,128)S(1)}, f32[8,32,128]{2,1,0:T(8,128)S(1)}, f32[32,128]{1,0:T(8,128)S(1)}, f32[4,64,16,64]{3,2,1,0:T(8,128)S(1)}, ...) custom-call(f32[64,32,128]{2,1,0:T(8,128)} %field.1, ...), custom_call_target="tpu_custom_call" | custom-call | tf_op jit(solution)/shard_map/pallas_call | solution.py:454
  66.6 1.8 %shard_map.129 = (f32[64,32,128]{2,1,0:T(8,128)}, f32[64,16,64]{2,1,0:T(8,128)}, f32[3,64,16,64]{3,2,1,0:T(8,128)}, f32[64,64]{1,0:T(8,128)}, f32[1,64]{1,0:T(1,128)}) custom-call(f32[16,128,128]{2,1,0:T(8,128)S(1)} %get-tuple-element.18.base, f32[8,32,128]{2,1,0:T(8,128)S(1)} %get-tuple-element.19.recv4, f32[32,128]{1,0:T(8,128)S(1)} %get-tuple-element.20.send4, ...), custom_call_target="tpu_custom_call" | custom-call | tf_op jit(solution)/shard_map/pallas_call | solution.py:520

commit v3 on v2

--- a/solution.py
+++ b/solution.py
@@ -77,6 +77,9 @@
     return lat, split, join
 
 
+USED = (tables()[0].reshape(PAIRS, 4, 4, 2 * C) != 0).any(axis=3).tolist()
+
+
 def halves(x):
     high = x.astype(BF16)
     return high, (x - high.astype(F32)).astype(BF16)
@@ -122,16 +125,16 @@
     field, cot, wa, wd, wpoint, bias, lat_hbm, split_hbm, join_hbm,
     base, recv4, send4, out_gw, out_gp, out_gb, lat_tab, join_tab,
     fbuf, cbuf, wbuf, wpbuf, biasbuf, split_tab,
-    wfwd, wbwd, grad, thl, ghl, yscr, dup,
+    wmix, wfwd, wbwd, grad, thl, ghl, yscr, dup,
     send1, send2, send3, recv1, recv2, recv3, coarse,
-    red1, red2, red3, red4, red5,
+    red1, red2, red3, red4,
     load_sem, fload_sem, send_sem, recv_sem, rsend_sem, rrecv_sem,
 ):
     lat_at = lax.axis_index("lat")
     lon_at = lax.axis_index("lon")
     left = lax.broadcasted_iota(jnp.int32, (32, 2 * C), 1) < C
 
-    steps = [(0, 1), (1, 1), (2, 1), (3, 1), (3, 0), (2, 0), (1, 0)]
+    steps = [(2, 1), (1, 1), (3, 1), (0, 1), (2, 0), (1, 0), (3, 0)]
     behind = [(lax.rem(lat_at + (LAT - dl), LAT), lax.rem(lon_at + (LON - ds), LON)) for dl, ds in steps]
     ahead = [(lax.rem(lat_at + dl, LAT), lax.rem(lon_at + ds, LON)) for dl, ds in steps]
     zhi = lon_at // 8
@@ -145,16 +148,17 @@
         return (lax.rem(z_run, 2) * 16 + z_inner * 4 + y_at, (z_run // 2) * 8 + lax.rem(lon_at, 8))
 
     turns = [lambda i, d=d: lax.rem(i + d, 4) for d in (2, 1, 3)]
+    same_core = [(zlo * 4 + t(y_at), lon_at) for t in turns]
+    other_core = [(zlo * 4 + t(y_at), lon_at + 1 - 2 * core) for t in turns]
     sum_steps = [
-        (core, [(lat_at, lon_at + 1 - 2 * core)]),
-        (y_at, [(zlo * 4 + t(y_at), lon_at) for t in turns]),
+        (core * 4 + y_at, same_core + other_core + [(lat_at, lon_at + 1 - 2 * core)]),
         (x_at, [(lat_at, zhi * 8 + t(x_at) * 2 + core) for t in turns]),
         (inner, [at(run, t(inner)) for t in turns]),
         (run, [at(t(run), inner) for t in turns]),
     ]
 
     barrier = pltpu.get_barrier_semaphore()
-    everyone = sum_steps[4][1] + behind + ahead + sum_steps[3][1] + sum_steps[2][1]
+    everyone = sum_steps[3][1] + behind + ahead + sum_steps[2][1] + sum_steps[1][1] + other_core
 
     field_loads = [
         pltpu.make_async_copy(field.at[:, pl.ds(8 * q, 8), :], fbuf.at[q], fload_sem.at[q]) for q in range(4)
@@ -187,25 +191,23 @@
         yscr[at, :, :] = sums[:, :128]
         yscr[at + 1, :, :] = sums[:, 128:]
 
-    def lat_split(buffer, on_block):
-        for dl in (3, 2, 1, 0):
-            def step(g, sums, dl=dl):
-                sums = list(sums)
-                for n in range(4):
-                    h2 = g * 4 + n
-                    y = yscr[h2]
-                    for m in range(4):
-                        sums[m] = sums[m] + lat_tab[pl.ds(h2 * 16 + dl * 4 + m, 1), :] * y
-                return tuple(sums)
-
-            zero = jnp.zeros((32, 2 * C), F32)
-            sums = lax.fori_loop(0, 4, step, (zero,) * 4)
+    def lat_split(buffer, send):
+        for dl in (2, 1, 3, 0):
+            sums = [None] * 4
+            for h2 in range(PAIRS):
+                y = yscr[h2]
+                for m in range(4):
+                    if USED[h2][dl][m]:
+                        term = lat_tab[pl.ds(h2 * 16 + dl * 4 + m, 1), :] * y
+                        sums[m] = term if sums[m] is None else sums[m] + term
             for u in range(2):
                 first, second = sums[2 * u], sums[2 * u + 1]
                 modes = jnp.where(left, first, second) + swap(jnp.where(left, second, first))
                 for ds in range(2):
                     buffer[dl * 2 + ds, u * 16:(u + 1) * 16, :] = modes[ds * 16:(ds + 1) * 16]
-            on_block(dl)
+            send(dl, 1)
+        for dl in (2, 1, 3):
+            send(dl, 0)
 
     def exchange(number, source_of, recv, targets):
         return [
@@ -220,13 +222,6 @@
             for n, (dl, ds) in enumerate(steps)
         ]
 
-    def start_block(copies):
-        def on_block(dl):
-            for n, step in enumerate(steps):
-                if step[0] == dl:
-                    copies[n].start()
-        return on_block
-
     def point_map(weights, rows):
         high = [rows[64 * n:64 * n + 64, :W] for n in range(4)]
         rest = [rows[64 * n:64 * n + 64, W:] for n in range(4)]
@@ -246,9 +241,11 @@
                 thl[(h2 + k) * 128:(h2 + k + 1) * 128, W:] = rest
             lon_split(thl[h2 * 128:h2 * 128 + 256, :], h2)
     lat_load.wait()
+    lat_split(send1, lambda dl, ds: None)
     pl.semaphore_wait(barrier, len(everyone))
     copies1 = exchange(0, lambda n: send1.at[n], recv1, behind)
-    lat_split(send1, start_block(copies1))
+    for copy in copies1:
+        copy.start()
 
     wp_load.wait()
     bias_load.wait()
@@ -266,27 +263,46 @@
     wa_load.wait()
     wd_load.wait()
 
+    def prepare(b, carry):
+        flat = wbuf.at[b].reshape(C * 16, C)
+        for n in range(16):
+            one = flat[pl.ds(n, C, stride=16), :]
+            high = one.astype(BF16).astype(F32)
+            wmix[b * 16 + n] = jnp.concatenate([high, one - high], 1).astype(BF16)
+        return carry
+
+    lax.fori_loop(0, 4, prepare, 0)
+
     total = send1[0]
     for n, (dl, ds) in enumerate(steps):
         copies1[n].wait_recv()
         total = total + recv1[dl * 2 + ds]
     coarse[...] = total
 
-    def mix(g, carry):
-        turned, sums = carry
-        sums = list(sums)
-        for k in range(8):
-            for b in range(4):
-                rows = turned[8 * b:8 * b + 8]
-                column = jnp.concatenate([rows[:, k:k + 1], rows[:, C + k:C + k + 1]], 0)
-                sums[b] = sums[b] + column * wbuf[b, g * 8 + k]
-        return pltpu.roll(turned, 2 * C - 8, axis=1), tuple(sums)
-
-    def packed(parts):
-        return jnp.concatenate([jnp.concatenate([p[:8], p[8:]], 1) for p in parts], 0)
-
-    _, mixed = lax.fori_loop(0, C // 8, mix, (total, (jnp.zeros((16, C), F32),) * 4))
-    send2[...] = packed(mixed) - total
+    row8 = lax.broadcasted_iota(jnp.int32, (8, 2 * C), 0)
+    half8 = lax.broadcasted_iota(jnp.int32, (8, 2 * C), 1) // C
+    left8 = half8 == 0
+
+    def stacked(x):
+        high = x.astype(BF16).astype(F32)
+        return jnp.concatenate([high, x - high], 0).astype(BF16)
+
+    mixed = []
+    for b in range(4):
+        both = []
+        for ii in range(2):
+            rows = total[8 * b:8 * b + 8]
+            lhs = stacked((rows if ii == 0 else swap(rows))[:, :C])
+            kept = jnp.zeros((8, 2 * C), F32)
+            for j2 in range(4):
+                at = b * 16 + ii * 8 + j2 * 2
+                out = jnp.dot(lhs, jnp.concatenate([wmix[at], wmix[at + 1]], 1), preferred_element_type=F32)
+                out = out[:8] + out[8:]
+                kept = jnp.where(row8 == 2 * j2, out[:, :128], kept)
+                kept = jnp.where(row8 == 2 * j2 + 1, out[:, 128:], kept)
+            both.append(kept + swap(kept))
+        mixed.append(jnp.where(left8, both[0], both[1]))
+    send2[...] = jnp.concatenate(mixed, 0) - total
     copies2 = exchange(1, lambda n: send2, recv2, ahead)
     for copy in copies2:
         copy.start()
@@ -298,17 +314,18 @@
         copy.wait_recv()
     lat_join(recv2, send2, dup, left)
 
+    for h2 in range(PAIRS):
+        base[h2] = base[h2] + lon_join(h2, dup, lat_tab, join_tab)
+    for h2 in range(PAIRS):
+        g = gelu_slope(base[h2]) * cell_pair(cbuf, h2)
+        grad[h2] = g
+        high, rest = halves(g)
+        ghl[h2 * 128:(h2 + 1) * 128, :W] = high
+        ghl[h2 * 128:(h2 + 1) * 128, W:] = rest
     for h4 in range(PAIRS // 2):
-        for k in range(2):
-            h2 = 2 * h4 + k
-            g = gelu_slope(base[h2] + lon_join(h2, dup, lat_tab, join_tab)) * cell_pair(cbuf, h2)
-            grad[h2] = g
-            high, rest = halves(g)
-            ghl[h2 * 128:(h2 + 1) * 128, :W] = high
-            ghl[h2 * 128:(h2 + 1) * 128, W:] = rest
         lon_split(ghl[h4 * 256:h4 * 256 + 256, :], 2 * h4)
     copies3 = exchange(2, lambda n: send3.at[n], recv3, behind)
-    lat_split(send3, start_block(copies3))
+    lat_split(send3, lambda dl, ds: copies3[steps.index((dl, ds))].start())
 
     point = jnp.zeros((128, 128), F32)
     rows_sum = jnp.zeros((C, W), F32)
@@ -324,7 +341,7 @@
     point = point[:C] + point[C:]
     point = point + swap(point)
     bias_term = jnp.sum(rows_sum, axis=1, keepdims=True)
-    sums_of = [red1, red2, red3, red4, red5]
+    sums_of = [red1, red2, red3, red4]
     folded = jnp.concatenate([point[: C // 2, :C], point[C // 2:, :C]], 1)
     bias_row = jnp.broadcast_to(bias_term, (C, 128)).T[:8]
     first = jnp.concatenate([folded, jnp.concatenate([bias_row, bias_row], 1)], 0)
@@ -367,7 +384,6 @@
             base[h2] = mapped[128 * k:128 * k + 128] + grad[h2]
     send_sum(1, take_sum(0))
     send_sum(2, take_sum(1))
-    send_sum(3, take_sum(2))
 
     gtotal = send3[0]
     for n, (dl, ds) in enumerate(steps):
@@ -379,23 +395,28 @@
         return jnp.concatenate([part[:, :C], part[:, C:]], 0)
 
     gmodes = [unpacked(gtotal, b) for b in range(4)]
-    lanes16 = lax.broadcasted_iota(jnp.int32, (16, C), 1)
-
-    def back(g, sums):
-        sums = list(sums)
-        for k in range(8):
-            for b in range(4):
-                one = jnp.sum(wbuf[b, g * 8 + k] * gmodes[b], axis=1, keepdims=True)
-                sums[b] = jnp.where(lanes16 == g * 8 + k, one, sums[b])
-        return tuple(sums)
-
-    backs = lax.fori_loop(0, C // 8, back, (jnp.zeros((16, C), F32),) * 4)
-    send4[...] = packed(backs) - gtotal
+    backs = []
+    for b in range(4):
+        rows = gtotal[8 * b:8 * b + 8]
+        turned = swap(rows)
+        both = []
+        for ii in range(2):
+            lhs = stacked(jnp.where(left8, rows, turned) if ii == 0 else jnp.where(left8, turned, rows))
+            maps = wmix[b * 16 + ii * 8:b * 16 + ii * 8 + 8].reshape(8 * C, 2 * C)
+            out = dot_nt(lhs, maps)
+            out = out[:8] + out[8:]
+            kept = jnp.zeros((8, 2 * C), F32)
+            for j2 in range(4):
+                part = out[:, 128 * j2:128 * j2 + 128]
+                kept = jnp.where(row8 - half8 == 2 * j2, part, kept)
+            both.append(kept + swap(kept))
+        backs.append(jnp.where(left8, both[0], both[1]))
+    send4[...] = jnp.concatenate(backs, 0) - gtotal
     copies4 = exchange(3, lambda n: send4, recv4, ahead)
     for copy in copies4:
         copy.start()
 
-    send_sum(4, take_sum(3))
+    send_sum(3, take_sum(2))
 
     def outer(g, turned):
         for k in range(8):
@@ -408,7 +429,7 @@
     lax.fori_loop(0, C // 8, outer, coarse[...])
     for copy in copies4:
         copy.wait_recv()
-    rows = take_sum(4)
+    rows = take_sum(3)
     out_gp[...] = jnp.concatenate([rows[: C // 2, :C], rows[: C // 2, C:]], 0)
     out_gb[...] = rows[C // 2:C // 2 + 1, :C]
     for copy in copies1 + copies2 + copies3 + copies4 + sum(reduces, []):
@@ -472,6 +493,7 @@
             vmem((C, C), F32),
             vmem((1, C), F32),
             vmem((64, 2 * W), F32),
+            vmem((C, C, 2 * C), BF16),
             vmem((3 * C, C), BF16),
             vmem((3 * C, C), BF16),
             vmem((PAIRS, 2 * C, W), F32),
@@ -486,8 +508,7 @@
             vmem((8,) + block, F32),
             vmem((8,) + block, F32),
             vmem(block, F32),
-            vmem((2, 40, 128), F32),
-            vmem((4, 40, 128), F32),
+            vmem((8, 40, 128), F32),
             vmem((4, 40, 128), F32),
             vmem((4, 40, 128), F32),
             vmem((4, 40, 128), F32),
@@ -495,8 +516,8 @@
             pltpu.SemaphoreType.DMA((8,)),
             pltpu.SemaphoreType.DMA((4, 7)),
             pltpu.SemaphoreType.DMA((4, 7)),
-            pltpu.SemaphoreType.DMA((5, 3)),
-            pltpu.SemaphoreType.DMA((5, 3)),
+            pltpu.SemaphoreType.DMA((4, 7)),
+            pltpu.SemaphoreType.DMA((4, 7)),
         ],
         compiler_params=pltpu.CompilerParams(
             collective_id=0, has_side_effects=True, vmem_limit_bytes=48 * 1024 * 1024

time: 68.5 us -> 65.5 us (0.956)
  the two profiles are of different devices: /device:TPU:64 before, /device:TPU:32 now
where the time goes in v3:
time: 65.5 us; the launch traced here: 65.4 us
  Pallas kernels  64.8 us (99%)
    pallas_call x1, Pallas kernels, body(): pl.pallas_call(kernel, out_shape=(vmem((PAIRS, 2 * C, W), F32), vmem((8,)...  63 us
    pallas_call x1, Pallas kernels, body(): pl.pallas_call(last_kernel, out_shape=(jax.ShapeDtypeStruct((C, H, W), F3...  1.76 us

profile of v3, /device:TPU:32, one launch (start us, length us, event | category | flops | bytes accessed | tf_op | source)
XLA Modules:
  0.0 65.4 jit_solution(16614885298751793473)
XLA Ops:
  0.6 63.0 %shard_map.128 = (f32[16,128,128]{2,1,0:T(8,128)S(1)}, f32[8,32,128]{2,1,0:T(8,128)S(1)}, f32[32,128]{1,0:T(8,128)S(1)}, f32[4,64,16,64]{3,2,1,0:T(8,128)S(1)}, ...) custom-call(f32[64,32,128]{2,1,0:T(8,128)} %field.1, ...), custom_call_target="tpu_custom_call" | custom-call | tf_op jit(solution)/shard_map/pallas_call | solution.py:475
  63.7 1.8 %shard_map.129 = (f32[64,32,128]{2,1,0:T(8,128)}, f32[64,16,64]{2,1,0:T(8,128)}, f32[3,64,16,64]{3,2,1,0:T(8,128)}, f32[64,64]{1,0:T(8,128)}, f32[1,64]{1,0:T(1,128)}) custom-call(f32[16,128,128]{2,1,0:T(8,128)S(1)} %get-tuple-element.18.base, f32[8,32,128]{2,1,0:T(8,128)S(1)} %get-tuple-element.19.recv4, f32[32,128]{1,0:T(8,128)S(1)} %get-tuple-element.20.send4, ...), custom_call_target="tpu_custom_call" | custom-call | tf_op jit(solution)/shard_map/pallas_call | solution.py:541

commit v4 on v3

--- a/solution.py
+++ b/solution.py
@@ -151,14 +151,17 @@
     same_core = [(zlo * 4 + t(y_at), lon_at) for t in turns]
     other_core = [(zlo * 4 + t(y_at), lon_at + 1 - 2 * core) for t in turns]
     sum_steps = [
+        (run, [at(t(run), inner) for t in turns]),
+        (inner, [at(run, t(inner)) for t in turns]),
+        (x_at, [(lat_at, zhi * 8 + t(x_at) * 2 + core) for t in turns]),
         (core * 4 + y_at, same_core + other_core + [(lat_at, lon_at + 1 - 2 * core)]),
-        (x_at, [(lat_at, zhi * 8 + t(x_at) * 2 + core) for t in turns]),
-        (inner, [at(run, t(inner)) for t in turns]),
-        (run, [at(t(run), inner) for t in turns]),
     ]
 
     barrier = pltpu.get_barrier_semaphore()
-    everyone = sum_steps[3][1] + behind + ahead + sum_steps[2][1] + sum_steps[1][1] + other_core
+    everyone = ahead + behind + sum_steps[0][1] + sum_steps[1][1] + sum_steps[2][1] + other_core
+
+    for device in everyone:
+        pl.semaphore_signal(barrier, inc=1, device_id=device, device_id_type=MESH)
 
     field_loads = [
         pltpu.make_async_copy(field.at[:, pl.ds(8 * q, 8), :], fbuf.at[q], fload_sem.at[q]) for q in range(4)
@@ -177,8 +180,6 @@
     join_load = pltpu.make_async_copy(join_hbm, join_tab, load_sem.at[6])
     for load in [split_load, lat_load, wp_load, bias_load, wa_load, wd_load, join_load] + cot_loads:
         load.start()
-    for device in everyone:
-        pl.semaphore_signal(barrier, inc=1, device_id=device, device_id_type=MESH)
 
     def cell_pair(buffer, h2):
         chunk, row = h2 // 4, (h2 % 4) * 2
@@ -382,8 +383,6 @@
         for k in range(2):
             h2 = 2 * h4 + k
             base[h2] = mapped[128 * k:128 * k + 128] + grad[h2]
-    send_sum(1, take_sum(0))
-    send_sum(2, take_sum(1))
 
     gtotal = send3[0]
     for n, (dl, ds) in enumerate(steps):
@@ -416,7 +415,7 @@
     for copy in copies4:
         copy.start()
 
-    send_sum(3, take_sum(2))
+    send_sum(1, take_sum(0))
 
     def outer(g, turned):
         for k in range(8):
@@ -427,6 +426,8 @@
         return pltpu.roll(turned, 2 * C - 8, axis=1)
 
     lax.fori_loop(0, C // 8, outer, coarse[...])
+    send_sum(2, take_sum(1))
+    send_sum(3, take_sum(2))
     for copy in copies4:
         copy.wait_recv()
     rows = take_sum(3)
@@ -508,10 +509,10 @@
             vmem((8,) + block, F32),
             vmem((8,) + block, F32),
             vmem(block, F32),
-            vmem((8, 40, 128), F32),
             vmem((4, 40, 128), F32),
             vmem((4, 40, 128), F32),
             vmem((4, 40, 128), F32),
+            vmem((8, 40, 128), F32),
             pltpu.SemaphoreType.DMA((7,)),
             pltpu.SemaphoreType.DMA((8,)),
             pltpu.SemaphoreType.DMA((4, 7)),

time: 65.5 us -> 67 us (1.023)
  the two profiles are of different devices: /device:TPU:32 before, /device:TPU:64 now
where the time goes in v4:
time: 67 us; the launch traced here: 66.9 us
  Pallas kernels  66.2 us (99%)
    pallas_call x1, Pallas kernels, body(): pl.pallas_call(kernel, out_shape=(vmem((PAIRS, 2 * C, W), F32), vmem((8,)...  64.5 us
    pallas_call x1, Pallas kernels, body(): pl.pallas_call(last_kernel, out_shape=(jax.ShapeDtypeStruct((C, H, W), F3...  1.76 us

profile of v4, /device:TPU:64, one launch (start us, length us, event | category | flops | bytes accessed | tf_op | source)
XLA Modules:
  0.0 66.9 jit_solution(12813173901061417465)
XLA Ops:
  0.6 64.5 %shard_map.128 = (f32[16,128,128]{2,1,0:T(8,128)S(1)}, f32[8,32,128]{2,1,0:T(8,128)S(1)}, f32[32,128]{1,0:T(8,128)S(1)}, f32[4,64,16,64]{3,2,1,0:T(8,128)S(1)}, ...) custom-call(f32[64,32,128]{2,1,0:T(8,128)} %field.1, ...), custom_call_target="tpu_custom_call" | custom-call | tf_op jit(solution)/shard_map/pallas_call | solution.py:476
  65.1 1.8 %shard_map.129 = (f32[64,32,128]{2,1,0:T(8,128)}, f32[64,16,64]{2,1,0:T(8,128)}, f32[3,64,16,64]{3,2,1,0:T(8,128)}, f32[64,64]{1,0:T(8,128)}, f32[1,64]{1,0:T(1,128)}) custom-call(f32[16,128,128]{2,1,0:T(8,128)S(1)} %get-tuple-element.18.base, f32[8,32,128]{2,1,0:T(8,128)S(1)} %get-tuple-element.19.recv4, f32[32,128]{1,0:T(8,128)S(1)} %get-tuple-element.20.send4, ...), custom_call_target="tpu_custom_call" | custom-call | tf_op jit(solution)/shard_map/pallas_call | solution.py:542

commit v5 on v3

--- a/solution.py
+++ b/solution.py
@@ -158,7 +158,10 @@
     ]
 
     barrier = pltpu.get_barrier_semaphore()
-    everyone = sum_steps[3][1] + behind + ahead + sum_steps[2][1] + sum_steps[1][1] + other_core
+    everyone = ahead + behind + sum_steps[3][1] + sum_steps[2][1] + sum_steps[1][1] + other_core
+
+    for device in everyone:
+        pl.semaphore_signal(barrier, inc=1, device_id=device, device_id_type=MESH)
 
     field_loads = [
         pltpu.make_async_copy(field.at[:, pl.ds(8 * q, 8), :], fbuf.at[q], fload_sem.at[q]) for q in range(4)
@@ -177,8 +180,6 @@
     join_load = pltpu.make_async_copy(join_hbm, join_tab, load_sem.at[6])
     for load in [split_load, lat_load, wp_load, bias_load, wa_load, wd_load, join_load] + cot_loads:
         load.start()
-    for device in everyone:
-        pl.semaphore_signal(barrier, inc=1, device_id=device, device_id_type=MESH)
 
     def cell_pair(buffer, h2):
         chunk, row = h2 // 4, (h2 % 4) * 2

time: 65.5 us -> 65.9 us (level)
  no operation moved by 1% of the time
where the time goes in v5:
time: 65.9 us; the launch traced here: 65.7 us
  Pallas kernels  65.1 us (99%)
    pallas_call x1, Pallas kernels, body(): pl.pallas_call(kernel, out_shape=(vmem((PAIRS, 2 * C, W), F32), vmem((8,)...  63.3 us
    pallas_call x1, Pallas kernels, body(): pl.pallas_call(last_kernel, out_shape=(jax.ShapeDtypeStruct((C, H, W), F3...  1.76 us

profile of v5, /device:TPU:32, one launch (start us, length us, event | category | flops | bytes accessed | tf_op | source)
XLA Modules:
  0.0 65.7 jit_solution(5643626597254258903)
XLA Ops:
  0.6 63.3 %shard_map.128 = (f32[16,128,128]{2,1,0:T(8,128)S(1)}, f32[8,32,128]{2,1,0:T(8,128)S(1)}, f32[32,128]{1,0:T(8,128)S(1)}, f32[4,64,16,64]{3,2,1,0:T(8,128)S(1)}, ...) custom-call(f32[64,32,128]{2,1,0:T(8,128)} %field.1, ...), custom_call_target="tpu_custom_call" | custom-call | tf_op jit(solution)/shard_map/pallas_call | solution.py:476
  64.0 1.8 %shard_map.129 = (f32[64,32,128]{2,1,0:T(8,128)}, f32[64,16,64]{2,1,0:T(8,128)}, f32[3,64,16,64]{3,2,1,0:T(8,128)}, f32[64,64]{1,0:T(8,128)}, f32[1,64]{1,0:T(1,128)}) custom-call(f32[16,128,128]{2,1,0:T(8,128)S(1)} %get-tuple-element.18.base, f32[8,32,128]{2,1,0:T(8,128)S(1)} %get-tuple-element.19.recv4, f32[32,128]{1,0:T(8,128)S(1)} %get-tuple-element.20.send4, ...), custom_call_target="tpu_custom_call" | custom-call | tf_op jit(solution)/shard_map/pallas_call | solution.py:542
